TPU v7x, 512 devices: a whole 4x8x8 slice. The times are simulated.
512 devices in a mesh: sec: 2 (over core), blk: 128 (over x, y, z_lo), lev: 2 (over z_hi).
Axes of the slice: x: 4, y: 8, z: 8 (z_hi: 2, z_lo: 4; z = z_hi * 4 + z_lo), core: 2. Of those that a mesh axis runs over, the one named last changes fastest.
Arguments:
- state: float32 [1024, 32, 1536], P('blk', 'sec', 'lev'), may hold values from -6 to 6
- u_wind: float32 [1024, 32, 128], P('blk', 'sec', 'lev'), may hold values from -4 to 4
- v_wind: float32 [1024, 32, 128], P('blk', 'sec', 'lev'), may hold values from -4 to 4
- mixing: float32 [128, 128], replicated, may hold values from -1 to 2
- stretch_order: int32 [32768], P(('sec', 'blk')), may hold values from 0 to 127, as said below
- remap_index: int32 [65536, 4], P(('sec', 'blk', 'lev')), may hold values from 0 to 127
- remap_weight: float32 [65536, 4], P(('sec', 'blk', 'lev')), may hold values from 0.1 to 1
- land_sea: int32 [65536], P(('sec', 'blk', 'lev')), may hold values 0 or 1
- ocean_temp: float32 [80, 65536], P(None, ('sec', 'blk', 'lev')), may hold values from -6 to 6
- ocean_mixing: float32 [80, 80], replicated, may hold values from -1 to 2
Outputs:
- advanced_model_quantities: float32 [1024, 32, 1536], P('blk', 'sec', 'lev')
- parameterized_rate_per_line: float32 [32768, 128], P(('sec', 'blk', 'lev'))
- physics_row_fields: float32 [32768, 1536], P(('sec', 'blk', 'lev'))
- refreshed_sea_depth_curves: float32 [80, 65536], P(None, ('sec', 'blk', 'lev'))
- sst_atm: float32 [1024, 32], P('blk', 'sec')
Inputs may be any that keep to these rules, and one draw needn't show every extreme that they name: `stretch_order`: each aligned block of 128 entries is a permutation of 0 to 127.
All inputs are finite; a program needn't handle non-finite values. No bound on the sum of `land_sea` on one device may be relied on, other than what follows from the above.
Results may differ from a plain program's by a relative error of at most 0.0001.
Values sent between devices are 32-bit elements; how exact they have to be, the bound alone decides.
A program may use at most 64 MiB of HBM per device.

v0:
```python
import math

import jax
import jax.numpy as jnp
import numpy as np
from jax import lax
from jax.sharding import PartitionSpec as P

NP = 4
LEV = 128
NF = 12


HIGH = lax.Precision.HIGHEST


def padded_2(cells, sides, width):
    for axis, dim in sides:
        count = lax.axis_size(axis)
        head = lax.slice_in_dim(cells, 0, width, axis=dim)
        tail = lax.slice_in_dim(cells, cells.shape[dim] - width, cells.shape[dim], axis=dim)
        cells = jnp.concatenate(
            [
                lax.ppermute(tail, axis, [(i, (i + 1) % count) for i in range(count)]),
                cells,
                lax.ppermute(head, axis, [((i + 1) % count, i) for i in range(count)]),
            ],
            axis=dim,
        )
    return cells


def swapped(block, axis, stride):
    count = lax.axis_size(axis)
    route = []
    for low in range(count):
        high = low | 1 << stride
        if high != low and high < count:
            route += [(low, high), (high, low)]
    return lax.ppermute(block, axis, route)


def gll_derivative():
    nodes = np.array([-1.0, -1.0 / math.sqrt(5.0), 1.0 / math.sqrt(5.0), 1.0])
    count = nodes.shape[0]
    bary = np.ones(count)
    for j in range(count):
        for k in range(count):
            if k != j:
                bary[j] = bary[j] / (nodes[j] - nodes[k])
    table = np.zeros((count, count))
    for i in range(count):
        for j in range(count):
            if i != j:
                table[i, j] = bary[j] / bary[i] / (nodes[i] - nodes[j])
        table[i, i] = -np.sum(table[i])
    return table.astype(np.float32)


def substep(field, u_rep, v_rep, deriv_table, sec_index):
    lengthwise_extent, transverse_extent, chans = field.shape
    along_x = field.reshape(lengthwise_extent // NP, NP, transverse_extent, chans)
    diff_x = jnp.einsum("ij,ejyc->eiyc", deriv_table, along_x, precision=HIGH).reshape(field.shape)
    along_y = field.reshape(lengthwise_extent, transverse_extent // NP, NP, chans)
    diff_y = jnp.einsum("ij,xejc->xeic", deriv_table, along_y, precision=HIGH).reshape(field.shape)
    field = field - 0.1 * (u_rep * diff_x + v_rep * diff_y)
    padded = padded_2(field, (("blk", 0),), 1)
    blocks = field.reshape(lengthwise_extent // NP, NP, transverse_extent, chans)
    lead_row = blocks[:, 0]
    tail_row = blocks[:, NP - 1]
    next_lead = jnp.concatenate([lead_row[1:], padded[-1:]], axis=0)
    prev_tail = jnp.concatenate([padded[:1], tail_row[:-1]], axis=0)
    avg_up = 0.5 * (tail_row + next_lead)
    avg_down = 0.5 * (prev_tail + lead_row)
    blocks = blocks.at[:, NP - 1].set(avg_up).at[:, 0].set(avg_down)
    field = blocks.reshape(field.shape)
    edge_row = jnp.where(sec_index == 0, field[:, -1], field[:, 0])
    received = swapped(edge_row, "sec", 0)
    blocks = field.reshape(lengthwise_extent, transverse_extent // NP, NP, chans)
    lead_row = blocks[:, :, 0]
    tail_row = blocks[:, :, NP - 1]
    next_lead = jnp.concatenate([lead_row[:, 1:], received[:, None]], axis=1)
    prev_tail = jnp.concatenate([received[:, None], tail_row[:, :-1]], axis=1)
    avg_up = 0.5 * (tail_row + next_lead)
    avg_down = 0.5 * (prev_tail + lead_row)
    last_up = jnp.where(sec_index == 0, avg_up[:, -1], tail_row[:, -1])
    first_down = jnp.where(sec_index == 1, avg_down[:, 0], lead_row[:, 0])
    new_tail = jnp.concatenate([avg_up[:, :-1], last_up[:, None]], axis=1)
    new_lead = jnp.concatenate([first_down[:, None], avg_down[:, 1:]], axis=1)
    blocks = blocks.at[:, :, NP - 1].set(new_tail).at[:, :, 0].set(new_lead)
    return blocks.reshape(field.shape)


def physics(stretch, mixing):
    rows = stretch.shape[0]
    cube = stretch.reshape(rows, LEV, NF)
    mixed = jnp.einsum("kj,cjf->ckf", mixing, cube, precision=HIGH)
    temper = mixed[:, :, 0]
    vapour = mixed[:, :, 2]
    condense = jnp.maximum(vapour - 0.5 * jnp.exp(0.3 * temper), 0.0)
    mixed = mixed.at[:, :, 0].set(temper + 0.5 * condense).at[:, :, 2].set(vapour - condense)
    return (mixed.reshape(rows, LEV * NF), condense)


def on_device(
    state,
    u_wind,
    v_wind,
    mixing,
    stretch_order,
    remap_index,
    remap_weight,
    land_sea,
    ocean_temp,
    ocean_mixing,
):
    lengthwise_extent, transverse_extent, chans = state.shape
    lev_dev = u_wind.shape[2]
    deriv_table = jnp.asarray(gll_derivative())
    sec_index = lax.axis_index("sec")
    lev_index = lax.axis_index("lev")
    u_rep = jnp.repeat(u_wind, NF, axis=2)
    v_rep = jnp.repeat(v_wind, NF, axis=2)
    field = state
    for turn in range(2):
        field = substep(field, u_rep, v_rep, deriv_table, sec_index)
    columns = field.reshape(lengthwise_extent * transverse_extent, chans)
    outgoing = jnp.take(columns, stretch_order, axis=0)
    stretch = lax.all_to_all(
        lax.all_to_all(outgoing, "blk", split_axis=0, concat_axis=0, tiled=True),
        "lev",
        split_axis=0,
        concat_axis=1,
        tiled=True,
    )
    physics_row_fields, parameterized_rate_per_line = physics(stretch, mixing)
    returned = lax.all_to_all(
        lax.all_to_all(physics_row_fields, "lev", split_axis=1, concat_axis=0, tiled=True),
        "blk",
        split_axis=0,
        concat_axis=0,
        tiled=True,
    )
    columns_new = jnp.zeros_like(columns).at[stretch_order].set(returned)
    advanced_model_quantities = columns_new.reshape(lengthwise_extent, transverse_extent, chans)
    level_pos = (lev_index * lev_dev + jnp.arange(lev_dev, dtype=jnp.int32)).astype(jnp.float32)
    level_weight = (1.0 + level_pos / LEV) / math.sqrt(LEV)
    cube = columns_new.reshape(lengthwise_extent * transverse_extent, lev_dev, NF)
    partial_flux = jnp.stack(
        [
            jnp.sum(cube[:, :, 0] * level_weight, axis=1),
            jnp.sum(cube[:, :, 2] * level_weight, axis=1),
        ]
    )
    fluxes = lax.psum(partial_flux, "lev")
    fluxes = swapped(fluxes, "sec", 0)
    sea = land_sea.astype(jnp.float32)
    picked = fluxes[:, remap_index]
    forcing = sea * jnp.sum(remap_weight * (0.5 * picked[0] + 0.5 * picked[1]), axis=1)
    lifted = ocean_temp.at[0].set(ocean_temp[0] + forcing)
    refreshed_sea_depth_curves = jnp.dot(
        ocean_mixing, lifted, precision=HIGH, preferred_element_type=jnp.float32
    )
    surface = refreshed_sea_depth_curves[0]
    broadcast_entries = (remap_weight * (sea * surface)[:, None]).reshape(-1)
    incomplete_skin_heat_share = jax.ops.segment_sum(
        broadcast_entries,
        remap_index.reshape(-1),
        num_segments=lengthwise_extent * transverse_extent,
    )
    skin_heat_per_vertical = lax.psum(incomplete_skin_heat_share, "lev")
    skin_heat_per_vertical = swapped(skin_heat_per_vertical, "sec", 0)
    return (
        advanced_model_quantities,
        parameterized_rate_per_line,
        physics_row_fields,
        refreshed_sea_depth_curves,
        skin_heat_per_vertical.reshape(lengthwise_extent, transverse_extent),
    )


def solution(mesh):
    placed = (
        P("blk", "sec", "lev"),
        P("blk", "sec", "lev"),
        P("blk", "sec", "lev"),
        P(),
        P(("sec", "blk")),
        P(("sec", "blk", "lev"), None),
        P(("sec", "blk", "lev"), None),
        P(("sec", "blk", "lev")),
        P(None, ("sec", "blk", "lev")),
        P(),
    )
    return jax.shard_map(
        on_device,
        mesh=mesh,
        in_specs=placed,
        out_specs=(
            P("blk", "sec", "lev"),
            P(("sec", "blk", "lev"), None),
            P(("sec", "blk", "lev"), None),
            P(None, ("sec", "blk", "lev")),
            P("blk", "sec"),
        ),
        check_vma=False,
    )
```

profile of v0, /device:TPU:1, one launch (start us, length us, event | category | flops | bytes accessed | tf_op | source)
XLA Modules:
  0.0 208.3 jit_solution(8829673046440231269)
XLA Ops:
  0.6 0.8 copy.303
  1.5 1.1 reshape.513
  2.6 2.0 convolution_bitcast_fusion.3
  4.6 1.5 convolution_bitcast_fusion.2
  6.1 0.1 reshape.514
  6.2 3.4 %broadcast_in_dim.46 = f32[8,16,64,12]{3,2,1,0:T(8,128)} broadcast(f32[8,16,64]{2,1,0:T(8,128)} %param.34), dimensions={0,1,2} | broadcast | bytes 425984 | tf_op jit(solution)/shard_map/broadcast_in_dim | solution.py:122
  9.6 4.9 %reshape.509 = f32[8,16,768]{2,1,0:T(8,128)S(1)} reshape(f32[8,16,64,12]{3,2,1,0:T(8,128)} %broadcast_in_dim.46) | data formatting | bytes 786432 | tf_op jit(solution)/shard_map/reshape | solution.py:122
  14.6 2.6 %broadcast_in_dim.47 = f32[8,16,64,12]{3,2,1,0:T(8,128)} broadcast(f32[8,16,64]{2,1,0:T(8,128)S(1)} %copy-done.3), dimensions={0,1,2} | broadcast | bytes 425984 | tf_op jit(solution)/shard_map/broadcast_in_dim | solution.py:123
  17.2 4.9 %reshape.512 = f32[8,16,768]{2,1,0:T(8,128)S(1)} reshape(f32[8,16,64,12]{3,2,1,0:T(8,128)} %broadcast_in_dim.47) | data formatting | bytes 786432 | tf_op jit(solution)/shard_map/reshape | solution.py:123
  22.1 0.1 fusion.12
  22.2 4.8 %collective-permute-start.1 = (f32[1,16,768]{2,1,0:T(8,128)S(1)}, f32[1,16,768]{2,1,0:T(8,128)S(1)}, u32[]{:S(2)}, u32[]{:S(2)}) collective-permute-start(f32[1,16,768]{2,1,0:T(8,128)S(1)} %get-tuple-element.173), channel_id=1, source_target_pairs={{0,2},{2,4},{4,6},{6,8},{8,10},{10,12},{12,14},{14,16},{16,18},{18... | collective-permute-start | bytes 147464 | tf_op jit(solution)/shard_map/ppermute | solution.py:24
  27.1 10.6 %collective-permute-start = (f32[1,16,768]{2,1,0:T(8,128)S(1)}, f32[1,16,768]{2,1,0:T(8,128)S(1)}, u32[]{:S(2)}, u32[]{:S(2)}) collective-permute-start(f32[1,16,768]{2,1,0:T(8,128)S(1)} %get-tuple-element.174), channel_id=1, source_target_pairs={{2,0},{4,2},{6,4},{8,6},{10,8},{12,10},{14,12},{16,14},{18,16},{20... | collective-permute-start | bytes 147464 | tf_op jit(solution)/shard_map/ppermute | solution.py:26
  37.8 4.9 %reshape.520 = f32[2,4,16,768]{3,2,1,0:T(8,128)S(1)} reshape(f32[8,16,64,12]{3,2,1,0:T(8,128)} %broadcast_in_dim.46) | data formatting | bytes 786432 | tf_op jit(solution)/shard_map/reshape | solution.py:122
  42.7 4.9 %reshape.521 = f32[2,4,16,768]{3,2,1,0:T(8,128)S(1)} reshape(f32[8,16,64,12]{3,2,1,0:T(8,128)} %broadcast_in_dim.47) | data formatting | bytes 786432 | tf_op jit(solution)/shard_map/reshape | solution.py:123
  48.0 5.4 %collective-permute-start.2 = (f32[8,768]{1,0:T(8,128)S(1)}, f32[8,768]{1,0:T(8,128)S(1)}, u32[]{:S(2)}, u32[]{:S(2)}) collective-permute-start(f32[8,768]{1,0:T(8,128)S(1)} %fusion.31), channel_id=1, source_target_pairs={{0,256},{256,0},{1,257},{257,1},{2,258},{258,2},{3,259},{259,3},{4... | collective-permute-start | bytes 73736 | tf_op jit(solution)/shard_map/ppermute | solution.py:40
  53.3 0.2 fusion.45
  53.6 0.4 collective-permute-done.2
  54.0 0.1 fusion.26
  54.6 2.1 %scatter.46 = f32[8,4,4,768]{3,2,1,0:T(4,128)S(1)} dynamic-update-slice(f32[8,4,4,768]{3,2,1,0:T(4,128)S(1)} %reshape_reshape.10, f32[8,4,1,768]{3,2,1,0:T(1,128)S(1)} %copy.222, s32[]{:T(128)} %constant.305.clone.1, s32[]{:T(128)} %constant.305.clone.1, s32[]{:T(128)} %constant.310.clone.1, s32[]{:T(128)} %constant.305.clone.1) | dynamic-update-slice | bytes 196612 | tf_op jit(solution)/shard_map/scatter | solution.py:90
  56.7 2.1 %scatter.49 = f32[8,4,4,768]{3,2,1,0:T(4,128)S(1)} dynamic-update-slice(f32[8,4,4,768]{3,2,1,0:T(4,128)S(1)} %scatter.46, f32[8,4,1,768]{3,2,1,0:T(1,128)S(1)} %reshape.518, s32[]{:T(128)} %constant.305.clone.1, s32[]{:T(128)} %constant.305.clone.1, s32[]{:T(128)} %constant.305.clone.1, s32[]{:T(128)} %constant.305.clone.1) | dynamic-update-slice | bytes 196612 | tf_op jit(solution)/shard_map/scatter | solution.py:90
  58.9 0.8 convolution_bitcast_fusion.1
  59.7 0.1 reshape.519
  59.8 0.1 reshape.523
  60.0 0.9 reshape.525
  60.8 0.1 reshape.522
  61.0 1.0 fusion.13
  62.1 1.1 fusion.6
  63.2 1.9 collective-permute-start.3
  65.2 0.2 fusion.9
  65.4 3.4 %collective-permute-start.4 = (f32[1,16,768]{2,1,0:T(8,128)S(1)}, f32[1,16,768]{2,1,0:T(8,128)S(1)}, u32[]{:S(2)}, u32[]{:S(2)}) collective-permute-start(f32[1,16,768]{2,1,0:T(8,128)S(1)} %get-tuple-element.165), channel_id=1, source_target_pairs={{0,2},{2,4},{4,6},{6,8},{8,10},{10,12},{12,14},{14,16},{16,18},{18... | collective-permute-start | bytes 147464 | tf_op jit(solution)/shard_map/ppermute | solution.py:24
  68.8 7.4 %collective-permute-done.4 = f32[1,16,768]{2,1,0:T(8,128)S(1)} collective-permute-done((f32[1,16,768]{2,1,0:T(8,128)S(1)}, f32[1,16,768]{2,1,0:T(8,128)S(1)}, u32[]{:S(2)}, u32[]{:S(2)}) %collective-permute-start.4) | collective-permute-done | bytes 49184 | tf_op jit(solution)/shard_map/ppermute | solution.py:24
  76.4 3.5 %collective-permute-start.5 = (f32[8,768]{1,0:T(8,128)S(1)}, f32[8,768]{1,0:T(8,128)S(1)}, u32[]{:S(2)}, u32[]{:S(2)}) collective-permute-start(f32[8,768]{1,0:T(8,128)S(1)} %fusion.30), channel_id=1, source_target_pairs={{0,256},{256,0},{1,257},{257,1},{2,258},{258,2},{3,259},{259,3},{4... | collective-permute-start | bytes 73736 | tf_op jit(solution)/shard_map/ppermute | solution.py:40
  79.9 0.2 fusion.41
  80.2 0.6 collective-permute-done.5
  80.8 0.1 fusion.28
  81.4 2.1 %scatter.54 = f32[8,4,4,768]{3,2,1,0:T(4,128)S(1)} dynamic-update-slice(f32[8,4,4,768]{3,2,1,0:T(4,128)S(1)} %reshape_reshape.11, f32[8,4,1,768]{3,2,1,0:T(1,128)S(1)} %copy.231, s32[]{:T(128)} %constant.305.clone.1, s32[]{:T(128)} %constant.305.clone.1, s32[]{:T(128)} %constant.310.clone.1, s32[]{:T(128)} %constant.305.clone.1) | dynamic-update-slice | bytes 196612 | tf_op jit(solution)/shard_map/scatter | solution.py:90
  83.5 2.1 %scatter.55 = f32[8,4,4,768]{3,2,1,0:T(4,128)S(1)} dynamic-update-slice(f32[8,4,4,768]{3,2,1,0:T(4,128)S(1)} %scatter.54, f32[8,4,1,768]{3,2,1,0:T(1,128)S(1)} %copy.232, s32[]{:T(128)} %constant.305.clone.1, s32[]{:T(128)} %constant.305.clone.1, s32[]{:T(128)} %constant.305.clone.1, s32[]{:T(128)} %constant.305.clone.1) | dynamic-update-slice | bytes 196612 | tf_op jit(solution)/shard_map/scatter | solution.py:90
  85.6 0.1 reshape_reshape.12
  85.8 0.8 gather_fusion
  86.7 0.4 copy.233
  87.1 20.7 %all_to_all.50 = f32[128,1,768]{2,1,0:T(1,128)S(1)} all-to-all(f32[128,1,768]{2,1,0:T(1,128)S(1)} %copy.233), channel_id=1, replica_groups=mesh['sec'=2,'blk'=128,'lev'=2] {'blk'}, dimensions={0} | all-to-all | bytes 786432 | tf_op jit(solution)/shard_map/all_to_all | solution.py:130
  107.9 15.5 %all_to_all.51 = f32[2,64,768]{2,1,0:T(8,128)S(1)} all-to-all(f32[2,64,768]{2,1,0:T(8,128)S(1)} %bitcast.152), channel_id=1, replica_groups=mesh['sec'=2,'blk'=128,'lev'=2] {'lev'}, dimensions={0} | all-to-all | bytes 786432 | tf_op jit(solution)/shard_map/all_to_all | solution.py:129
  123.4 0.3 copy.234
  123.7 1.5 convolution_bitcast_fusion
  125.3 0.5 copy.236
  125.9 0.2 copy.237
  126.2 11.0 %all_to_all.52 = f32[64,2,768]{2,0,1:T(8,128)S(1)} all-to-all(f32[64,2,768]{2,0,1:T(8,128)S(1)} %copy.237), channel_id=1, replica_groups=mesh['sec'=2,'blk'=128,'lev'=2] {'lev'}, dimensions={1} | all-to-all | bytes 786432 | tf_op jit(solution)/shard_map/all_to_all | solution.py:138
  137.2 1.2 copy.238
  138.3 16.6 %all-to-all-start.3 = ((f32[128,1,768]{2,1,0:T(1,128)}), f32[128,1,768]{2,1,0:T(1,128)S(1)}, u32[]{:S(2)}, u32[]{:S(2)}) async-start(f32[128,1,768]{2,1,0:T(1,128)} %copy.238), calls=%async_computation.3 | async-start | bytes 786432 | tf_op jit(solution)/shard_map/all_to_all | solution.py:137
  155.2 12.5 %all-to-all-done.3 = f32[128,1,768]{2,1,0:T(1,128)S(1)} async-done(((f32[128,1,768]{2,1,0:T(1,128)}), f32[128,1,768]{2,1,0:T(1,128)S(1)}, u32[]{:S(2)}, u32[]{:S(2)}) %all-to-all-start.3) | async-done | bytes 393248 | tf_op jit(solution)/shard_map/all_to_all | solution.py:137
  167.7 1.1 scatter_custom_fusion
  168.8 0.2 copy.240
  169.2 0.1 copy.241
  169.3 11.1 %psum.14 = f32[2,128]{0,1:T(8,128)S(1)} all-reduce(f32[2,128]{0,1:T(8,128)S(1)} %copy.241), channel_id=1, replica_groups=mesh['sec'=2,'blk'=128,'lev'=2] {'lev'}, use_global_device_ids=true, to_apply=%region_3.4 | all-reduce | flops 256 | bytes 2048 | tf_op jit(solution)/shard_map/psum | solution.py:155
  180.5 7.7 %collective-permute-start.6 = (f32[2,128]{0,1:T(8,128)S(1)}, f32[2,128]{0,1:T(8,128)S(1)}, u32[]{:S(2)}, u32[]{:S(2)}) collective-permute-start(f32[2,128]{0,1:T(8,128)S(1)} %psum.14), channel_id=1, source_target_pairs={{0,256},{256,0},{1,257},{257,1},{2,258},{258,2},{3,259},{259,3},{4... | collective-permute-start | bytes 3080 | tf_op jit(solution)/shard_map/ppermute | solution.py:40
  188.4 0.6 collective-permute-done.6
  189.1 1.0 gather_fusion.1
  190.3 0.2 convolution_bitcast_fusion.4
  190.8 4.1 %scatter_custom_fusion.1 = f32[128]{0:T(128)S(1)} fusion(s32[512]{0:T(512)S(1)} %reshape.564, f32[512]{0:T(512)S(1)} %reshape.566, f32[]{:T(128)} %constant.304.clone.1), kind=kCustom, calls=%fused_computation.89 | custom fusion | flops 512 | bytes 516 | tf_op jit(solution)/shard_map/scatter-add | solution.py:166
  194.8 7.7 %psum.15 = f32[128]{0:T(128)S(1)} all-reduce(f32[128]{0:T(128)S(1)} %scatter_custom_fusion.1), channel_id=1, replica_groups=mesh['sec'=2,'blk'=128,'lev'=2] {'lev'}, use_global_device_ids=true, to_apply=%region_6.7 | all-reduce | flops 128 | bytes 1024 | tf_op jit(solution)/shard_map/psum | solution.py:171
  202.5 3.4 %collective-permute-start.7 = (f32[128]{0:T(128)S(1)}, f32[128]{0:T(128)S(1)}, u32[]{:S(2)}, u32[]{:S(2)}) collective-permute-start(f32[128]{0:T(128)S(1)} %psum.15), channel_id=1, source_target_pairs={{0,256},{256,0},{1,257},{257,1},{2,258},{258,2},{3,259},{259,3},{4... | collective-permute-start | bytes 1544 | tf_op jit(solution)/shard_map/ppermute | solution.py:40
  206.0 0.6 fusion.57
  206.7 1.0 copy.246
  207.7 0.7 reshape.535
  (96 shorter events, 3.2 us)
Async XLA Ops:
  0.6 123.1 %copy-start = (f32[128,128]{1,0:T(8,128)S(1)}, f32[128,128]{1,0:T(8,128)}, u32[]{:S(2)}) copy-start(f32[128,128]{1,0:T(8,128)} %param.36) | copy-start | bytes 196612
  6.2 8.3 %copy-start.3 = (f32[8,16,64]{2,1,0:T(8,128)S(1)}, f32[8,16,64]{2,1,0:T(8,128)}, u32[]{:S(2)}) copy-start(f32[8,16,64]{2,1,0:T(8,128)} %param.35) | copy-start | bytes 98308
  14.5 7.6 %copy-start.1 = (f32[8,16,768]{2,1,0:T(8,128)S(1)}, f32[8,16,768]{2,1,0:T(8,128)}, u32[]{:S(2)}) copy-start(f32[8,16,768]{2,1,0:T(8,128)} %param.33) | copy-start | bytes 1179652
  17.2 20.6 %copy-start.10 = (s32[128]{0:T(128)S(1)}, s32[128]{0:T(128)}, u32[]{:S(2)}) copy-start(s32[128]{0:T(128)} %param.37) | copy-start | bytes 1540
  22.2 25.5 %collective-permute-start.1 = (f32[1,16,768]{2,1,0:T(8,128)S(1)}, f32[1,16,768]{2,1,0:T(8,128)S(1)}, u32[]{:S(2)}, u32[]{:S(2)}) collective-permute-start(f32[1,16,768]{2,1,0:T(8,128)S(1)} %get-tuple-element.173), channel_id=1, source_target_pairs={{0,2},{2,4},{4,6},{6,8},{8,10},{10,12},{12,14},{14,16},{16,18},{18... | collective-permute-start | bytes 147464 | tf_op jit(solution)/shard_map/ppermute | solution.py:24
  27.1 20.6 %collective-permute-start = (f32[1,16,768]{2,1,0:T(8,128)S(1)}, f32[1,16,768]{2,1,0:T(8,128)S(1)}, u32[]{:S(2)}, u32[]{:S(2)}) collective-permute-start(f32[1,16,768]{2,1,0:T(8,128)S(1)} %get-tuple-element.174), channel_id=1, source_target_pairs={{2,0},{4,2},{6,4},{8,6},{10,8},{12,10},{14,12},{16,14},{18,16},{20... | collective-permute-start | bytes 147464 | tf_op jit(solution)/shard_map/ppermute | solution.py:26
  42.7 16.1 %copy-start.6 = (f32[4,4,1,1]{1,0,3,2:T(4,128)S(1)}, f32[4,4,1,1]{1,0,3,2:T(4,128)}, u32[]{:S(2)}) copy-start(f32[4,4,1,1]{1,0,3,2:T(4,128)} %constant.330) | copy-start | bytes 196
  48.0 6.0 %collective-permute-start.2 = (f32[8,768]{1,0:T(8,128)S(1)}, f32[8,768]{1,0:T(8,128)S(1)}, u32[]{:S(2)}, u32[]{:S(2)}) collective-permute-start(f32[8,768]{1,0:T(8,128)S(1)} %fusion.31), channel_id=1, source_target_pairs={{0,256},{256,0},{1,257},{257,1},{2,258},{258,2},{3,259},{259,3},{4... | collective-permute-start | bytes 73736 | tf_op jit(solution)/shard_map/ppermute | solution.py:40
  63.2 5.5 %collective-permute-start.3 = (f32[1,16,768]{2,1,0:T(8,128)S(1)}, f32[1,16,768]{2,1,0:T(8,128)S(1)}, u32[]{:S(2)}, u32[]{:S(2)}) collective-permute-start(f32[1,16,768]{2,1,0:T(8,128)S(1)} %get-tuple-element.166), channel_id=1, source_target_pairs={{2,0},{4,2},{6,4},{8,6},{10,8},{12,10},{14,12},{16,14},{18,16},{20... | collective-permute-start | bytes 147464 | tf_op jit(solution)/shard_map/ppermute | solution.py:26
  65.4 10.9 %collective-permute-start.4 = (f32[1,16,768]{2,1,0:T(8,128)S(1)}, f32[1,16,768]{2,1,0:T(8,128)S(1)}, u32[]{:S(2)}, u32[]{:S(2)}) collective-permute-start(f32[1,16,768]{2,1,0:T(8,128)S(1)} %get-tuple-element.165), channel_id=1, source_target_pairs={{0,2},{2,4},{4,6},{6,8},{8,10},{10,12},{12,14},{14,16},{16,18},{18... | collective-permute-start | bytes 147464 | tf_op jit(solution)/shard_map/ppermute | solution.py:24
  76.4 4.3 %collective-permute-start.5 = (f32[8,768]{1,0:T(8,128)S(1)}, f32[8,768]{1,0:T(8,128)S(1)}, u32[]{:S(2)}, u32[]{:S(2)}) collective-permute-start(f32[8,768]{1,0:T(8,128)S(1)} %fusion.30), channel_id=1, source_target_pairs={{0,256},{256,0},{1,257},{257,1},{2,258},{258,2},{3,259},{259,3},{4... | collective-permute-start | bytes 73736 | tf_op jit(solution)/shard_map/ppermute | solution.py:40
  125.2 29.8 %copy-start.7 = (s32[128,4]{0,1:T(4,128)S(1)}, s32[128,4]{0,1:T(4,128)}, u32[]{:S(2)}) copy-start(s32[128,4]{0,1:T(4,128)} %param.38) | copy-start | bytes 6148
  125.9 64.3 %copy-start.8 = (f32[128,4]{0,1:T(4,128)S(1)}, f32[128,4]{0,1:T(4,128)}, u32[]{:S(2)}) copy-start(f32[128,4]{0,1:T(4,128)} %param.39) | copy-start | bytes 6148
  125.9 64.4 %copy-start.9 = (s32[128]{0:T(128)S(1)}, s32[128]{0:T(128)}, u32[]{:S(2)}) copy-start(s32[128]{0:T(128)} %param.40) | copy-start | bytes 1540
  125.9 64.4 %copy-start.4 = (f32[80,80]{1,0:T(8,128)S(1)}, f32[80,80]{1,0:T(8,128)}, u32[]{:S(2)}) copy-start(f32[80,80]{1,0:T(8,128)} %param.42) | copy-start | bytes 76804
  138.3 29.3 %all-to-all-start.3 = ((f32[128,1,768]{2,1,0:T(1,128)}), f32[128,1,768]{2,1,0:T(1,128)S(1)}, u32[]{:S(2)}, u32[]{:S(2)}) async-start(f32[128,1,768]{2,1,0:T(1,128)} %copy.238), calls=%async_computation.3 | async-start | bytes 786432 | tf_op jit(solution)/shard_map/all_to_all | solution.py:137
  168.8 39.5 %copy-start.2 = (f32[128,768]{1,0:T(8,128)}, f32[128,768]{1,0:T(8,128)S(1)}, u32[]{:S(2)}) copy-start(f32[128,768]{1,0:T(8,128)S(1)} %scatter_custom_fusion) | copy-start | bytes 1179652
  180.5 8.6 %collective-permute-start.6 = (f32[2,128]{0,1:T(8,128)S(1)}, f32[2,128]{0,1:T(8,128)S(1)}, u32[]{:S(2)}, u32[]{:S(2)}) collective-permute-start(f32[2,128]{0,1:T(8,128)S(1)} %psum.14), channel_id=1, source_target_pairs={{0,256},{256,0},{1,257},{257,1},{2,258},{258,2},{3,259},{259,3},{4... | collective-permute-start | bytes 3080 | tf_op jit(solution)/shard_map/ppermute | solution.py:40
  190.5 17.8 %copy-start.5 = (f32[80,128]{1,0:T(8,128)}, f32[80,128]{1,0:T(8,128)S(1)}, u32[]{:S(2)}) copy-start(f32[80,128]{1,0:T(8,128)S(1)} %convolution_bitcast_fusion.4) | copy-start | bytes 122884
  202.5 5.1 %collective-permute-start.7 = (f32[128]{0:T(128)S(1)}, f32[128]{0:T(128)S(1)}, u32[]{:S(2)}, u32[]{:S(2)}) collective-permute-start(f32[128]{0:T(128)S(1)} %psum.15), channel_id=1, source_target_pairs={{0,256},{256,0},{1,257},{257,1},{2,258},{258,2},{3,259},{259,3},{4... | collective-permute-start | bytes 1544 | tf_op jit(solution)/shard_map/ppermute | solution.py:40
where the time goes:
time: 209 us; the launch traced here: 208 us
  blocking collectives  66.1 us (32%)
  starting transfers between devices  57.3 us (27%)
  local copies, waits for them, and re-layouts  47.9 us (23%)
  waiting for transfers between devices  21.5 us (10%)
  other arithmetic  7.17 us (3%)
  matrix products  6.85 us (3%)
    all_to_all x1, blocking collectives, on_device(): lax.all_to_all(outgoing, 'blk', split_axis=0, concat_axis=0, tiled=True)  20.7 us
    ppermute x4, starting transfers between devices, swapped(): return lax.ppermute(block, axis, route)  19.9 us
    all_to_all x1, starting transfers between devices, on_device(): lax.all_to_all(lax.all_to_all(physics_row_fields, 'lev', split_axis=1, co...  16.6 us
    all_to_all x1, blocking collectives, on_device(): lax.all_to_all(lax.all_to_all(outgoing, 'blk', split_axis=0, concat_axis=...  15.5 us
    ppermute x2, starting transfers between devices, padded_2(): lax.ppermute(head, axis, [((i + 1) % count, i) for i in range(count)])  12.6 us
    all_to_all x1, waiting for transfers between devices, on_device(): lax.all_to_all(lax.all_to_all(physics_row_fields, 'lev', split_axis=1, co...  12.5 us
    psum x1, blocking collectives, on_device(): fluxes = lax.psum(partial_flux, 'lev')  11.1 us
    all_to_all x1, blocking collectives, on_device(): lax.all_to_all(physics_row_fields, 'lev', split_axis=1, concat_axis=0, ti...  11 us
  transfers between devices with their start and end apart: 9, of which 5 were waited for; matrix products, arithmetic and copies ran while one was open for 6% of the time, Pallas kernels for 0%

commit v1 on v0

v1 whole, which is shorter than its diff:
```python
import functools
import math

import jax
import jax.numpy as jnp
import numpy as np
from jax import lax
from jax.experimental import pallas as pl
from jax.experimental.pallas import tpu as pltpu
from jax.sharding import PartitionSpec as P

NP = 4
LEV = 128
NF = 12
NX, NY = 8, 16
COLS = NX * NY
HL = 64
CH = HL * NF
NBLK = 128
LANES = 128
NQ = CH // LANES
F32 = jnp.float32
BF16 = jnp.bfloat16
HIGH = lax.Precision.HIGHEST
MESH = pl.DeviceIdType.MESH


def gll_derivative():
    nodes = np.array([-1.0, -1.0 / math.sqrt(5.0), 1.0 / math.sqrt(5.0), 1.0])
    count = nodes.shape[0]
    bary = np.ones(count)
    for j in range(count):
        for k in range(count):
            if k != j:
                bary[j] = bary[j] / (nodes[j] - nodes[k])
    table = np.zeros((count, count))
    for i in range(count):
        for j in range(count):
            if i != j:
                table[i, j] = bary[j] / bary[i] / (nodes[i] - nodes[j])
        table[i, i] = -np.sum(table[i])
    return table.astype(np.float32)


def iota(shape, dim):
    return lax.broadcasted_iota(jnp.int32, shape, dim)


def split2(x):
    hi = x.astype(BF16)
    lo = (x - hi.astype(F32)).astype(BF16)
    return hi, lo


def dot(a, b):
    return jnp.dot(a, b, preferred_element_type=F32)


def dot3(a, b_hi, b_lo):
    hi, lo = split2(a)
    return dot(hi, b_hi) + dot(lo, b_hi) + dot(hi, b_lo)


def remote(src, dst, send, recv, device):
    return pltpu.make_async_remote_copy(
        src_ref=src, dst_ref=dst, send_sem=send, recv_sem=recv,
        device_id=device, device_id_type=MESH,
    )


def row(ref, r):
    return ref.at[pl.ds(r, 1)]


def advect(field_ref, uw_ref, vw_ref, out_ref, table):
    y8 = iota((8, LANES), 0)
    at = lax.rem(y8, NP)
    coefs = {}
    for d in range(-3, 4):
        c = jnp.zeros((8, LANES), F32)
        for i in range(NP):
            if 0 <= i + d < NP:
                c = jnp.where(at == i, F32(table[i, i + d]), c)
        coefs[d] = c[None]
    for q in range(NQ):
        lanes = slice(q * LANES, (q + 1) * LANES)
        for e in range(2):
            rows = slice(e * 64, (e + 1) * 64)
            f = field_ref[rows, lanes].reshape(NP, NY, LANES)
            dx = []
            for i in range(NP):
                acc = F32(table[i, 0]) * f[0]
                for j in range(1, NP):
                    acc = acc + F32(table[i, j]) * f[j]
                dx.append(acc[None])
            dx = jnp.concatenate(dx, axis=0).reshape(64, LANES)
            f8 = f.reshape(8, 8, LANES)
            dy = coefs[0] * f8
            for d in (-3, -2, -1, 1, 2, 3):
                dy = dy + coefs[d] * pltpu.roll(f8, (-d) % 8, axis=1)
            dy = dy.reshape(64, LANES)
            out_ref[rows, lanes] = f.reshape(64, LANES) - (
                uw_ref[rows, :] * dx + vw_ref[rows, :] * dy
            )


def average(a_ref, x_from_left, x_from_right, edge_ref, cor_l, cor_r, out_ref, s):
    y = iota((NY, LANES), 0)
    i = lax.rem(y, NP)
    at_edge = ((y == NY - 1) & (s == 0)) | ((y == 0) & (s == 1))
    closed = ((y == NY - 1) & (s == 1)) | ((y == 0) & (s == 0))
    inside = ((i == 0) | (i == NP - 1)) & jnp.logical_not(closed)
    for q in range(NQ):
        lanes = slice(q * LANES, (q + 1) * LANES)
        a = [a_ref[x * NY:(x + 1) * NY, lanes] for x in range(NX)]
        e = edge_ref[:, lanes]
        e = [e[x:x + 1] for x in range(NX)]
        a[0] = 0.5 * (a[0] + x_from_left[:, lanes])
        a[7] = 0.5 * (a[7] + x_from_right[:, lanes])
        a[3] = a[4] = 0.5 * (a[3] + a[4])
        e[0] = 0.5 * (e[0] + cor_l[0:1, lanes])
        e[7] = 0.5 * (e[7] + cor_r[0:1, lanes])
        e[3] = e[4] = 0.5 * (e[3] + e[4])
        for x in range(NX):
            f = a[x]
            up = pltpu.roll(f, NY - 1, axis=0)
            dn = pltpu.roll(f, 1, axis=0)
            nb = jnp.where(i == NP - 1, up, dn)
            nb = jnp.where(at_edge, jnp.broadcast_to(e[x], (NY, LANES)), nb)
            out_ref[x * NY:(x + 1) * NY, lanes] = jnp.where(inside, 0.5 * (f + nb), f)


def window_kernel(
    state_ref, u_ref, v_ref, mixing_ref, order_ref, index_ref, weight_ref, sea_ref, temp_ref, omix_ref,
    adv_ref, rate_ref, rows_ref, curves_ref, sst_ref,
    perm, perm_t, uw, vw, field, adv1, adv2, edge1, edge2, xl, xr, ye, cl, cr,
    gone, came, tv, flux_out, flux_in, sst_out, sst_in, back, home, mixed, spare,
    halo_send, halo_recv, tv_send, tv_recv, flux_send, flux_recv, sst_send, sst_recv,
    go_send, go_recv, back_send, back_recv,
):
    s, b, l = lax.axis_index("sec"), lax.axis_index("blk"), lax.axis_index("lev")
    table = gll_derivative()
    left, right = lax.rem(b + NBLK - 1, NBLK), lax.rem(b + 1, NBLK)
    half = b // 64
    low = lax.rem(b, 64)
    own = l == half

    barrier = pltpu.get_barrier_semaphore()

    def greet(device):
        pl.semaphore_signal(barrier, inc=1, device_id=device, device_id_type=MESH)

    near = [(s, left, l), (s, right, l), (1 - s, b, l), (1 - s, left, l), (1 - s, right, l), (s, b, 1 - l), (1 - s, b, 1 - l)]
    for device in near:
        greet(device)

    def greet_sources(i, carry):
        j = l * 64 + lax.rem(low + i, 64)
        greet((s, j, 0))
        greet((s, j, 1))
        return carry

    lax.fori_loop(0, 64, greet_sources, 0, unroll=8)

    for q in range(NQ):
        wide = (CH, LANES)
        to = iota(wide, 1) + q * LANES
        perm[:, q * LANES:(q + 1) * LANES] = jnp.where(
            iota(wide, 0) == lax.rem(to, HL) * NF + to // HL, F32(1), F32(0)
        ).astype(BF16)
        perm_t[:, q * LANES:(q + 1) * LANES] = jnp.where(
            to == lax.rem(iota(wide, 0), HL) * NF + iota(wide, 0) // HL, F32(1), F32(0)
        ).astype(BF16)
    hi, lo = split2(state_ref[...])
    field[...] = dot(hi, perm[...]) + dot(lo, perm[...])
    for ref, wind in ((uw, u_ref), (vw, v_ref)):
        w = F32(0.1) * wind[...]
        ref[...] = jnp.concatenate([w, w], axis=1)

    square = (COLS, COLS)
    hot_t = jnp.where(iota(square, 0) == order_ref[...], F32(1), F32(0))
    hot = hot_t.T.astype(BF16)
    hot_t = hot_t.astype(BF16)

    mt = mixing_ref[...].T
    lane = iota((HL, LANES), 1)
    blocks = []
    for li in range(2):
        part = mt[li * HL:(li + 1) * HL]
        turned = pltpu.roll(part, HL, axis=1)
        zero = jnp.zeros_like(part)
        blocks.append(jnp.concatenate([jnp.where(lane < HL, part, zero), jnp.where(lane < HL, turned, zero)], axis=1))
        blocks.append(jnp.concatenate([jnp.where(lane < HL, zero, turned), jnp.where(lane < HL, zero, part)], axis=1))
    pair_hi, pair_lo = split2(jnp.concatenate(blocks, axis=0))

    sea = sea_ref[...].astype(F32)
    weigh = jnp.zeros(square, F32)
    for m in range(4):
        weigh = weigh + jnp.where(iota(square, 0) == index_ref[m:m + 1, :], weight_ref[m:m + 1, :], F32(0))
    calm = jnp.dot(omix_ref[...], temp_ref[...], precision=HIGH, preferred_element_type=F32)

    advect(field, uw, vw, adv1, table)
    pl.semaphore_wait(barrier, len(near) + 128)

    sends = []
    for turn, (a, edge) in enumerate(((adv1, edge1), (adv2, edge2))):
        if turn == 1:
            advect(field, uw, vw, a, table)
        for x in range(NX):
            bottom, top = a[x * NY:x * NY + 1, :], a[(x + 1) * NY - 1:(x + 1) * NY, :]
            edge[x:x + 1, :] = jnp.where(s == 0, top, bottom)
        parts = (
            (a.at[pl.ds(0, NY)], xr.at[turn], (s, left, l)),
            (a.at[pl.ds(COLS - NY, NY)], xl.at[turn], (s, right, l)),
            (edge, ye.at[turn], (1 - s, b, l)),
            (row(edge, 0), cr.at[turn], (1 - s, left, l)),
            (row(edge, NX - 1), cl.at[turn], (1 - s, right, l)),
        )
        copies = [
            remote(src, dst, halo_send.at[turn, i], halo_recv.at[turn, i], device)
            for i, (src, dst, device) in enumerate(parts)
        ]
        for c in copies:
            c.start()
        for c in copies:
            c.wait_recv()
        sends += copies
        average(a, xl.at[turn], xr.at[turn], ye.at[turn], cl.at[turn], cr.at[turn], field, s)

    lane128 = iota((COLS, LANES), 1)
    tv[pl.ds(l, 1)] = jnp.where(
        lane128 < HL, field[:, 0:LANES], pltpu.roll(field[:, LANES:2 * LANES], HL, axis=1)
    )[None]
    tv_copy = remote(tv.at[l], tv.at[l], tv_send, tv_recv, (s, b, 1 - l))
    tv_copy.start()
    sends.append(tv_copy)

    hi, lo = split2(field[...])
    gone[...] = dot(hot, hi) + dot(hot, lo)
    slot = l * 64 + low
    bx, by, bz = b // 32, lax.rem(b // 4, 8), lax.rem(b, 4)

    def send_column(t, carry):
        dz, dx, dy = lax.rem(t, 4), lax.rem(t // 4, 4), t // 16
        p = lax.rem(bx + dx, 4) * 32 + lax.rem(by + dy, 8) * 4 + lax.rem(bz + dz, 4)
        remote(row(gone, p), row(came, slot), go_send, go_recv, (s, p, half)).start()
        return carry

    lax.fori_loop(1, 128, send_column, 0, unroll=8)

    @pl.when(own)
    def _():
        pltpu.make_async_copy(row(gone, b), row(came, slot), go_recv).start()
        pltpu.make_async_copy(row(gone, b), spare.at[0], go_send).start()

    @pl.when(jnp.logical_not(own))
    def _():
        send_column(0, 0)

    tv_copy.wait_recv()
    whole = jnp.concatenate([tv[0], tv[1]], axis=1)
    both = dot3(whole, pair_hi, pair_lo)
    level = lax.rem(lane128, HL)
    total = jnp.zeros((COLS, LANES), F32)
    for lo_ in range(2):
        part = both[:, lo_ * LANES:(lo_ + 1) * LANES]
        vapour = pltpu.roll(part, HL, axis=1)
        condense = jnp.maximum(vapour - 0.5 * jnp.exp(0.3 * part), 0.0)
        heat = part + 0.5 * condense
        moist = vapour - condense
        w = (1.0 + (level + lo_ * HL).astype(F32) / LEV) / math.sqrt(LEV)
        total = total + jnp.where(lane128 < HL, w * (0.5 * heat + 0.5 * moist), 0.0)
    flux = jnp.sum(total.T, axis=0, keepdims=True)
    flux_out[...] = jnp.broadcast_to(flux, (8, LANES))
    flux_copy = remote(flux_out, flux_in, flux_send, flux_recv, (1 - s, b, l))
    flux_copy.start()
    sends.append(flux_copy)

    flux_copy.wait_recv()
    forcing = jnp.dot(flux_in[...], weigh, precision=HIGH, preferred_element_type=F32)
    forcing = sea * forcing[0:1]
    curves = calm + omix_ref[:, 0:1] * forcing
    curves_ref[...] = curves
    entry = jnp.broadcast_to(sea * curves[0:1], (8, LANES))
    sst_out[...] = lax.dot_general(
        entry, weigh, (((1,), (1,)), ((), ())), precision=HIGH, preferred_element_type=F32
    )
    sst_copies = [
        remote(sst_out, sst_in.at[l], sst_send.at[k], sst_recv.at[l], (1 - s, b, k)) for k in range(2)
    ]
    for c in sst_copies:
        c.start()

    pltpu.make_async_copy(came, came, go_recv).wait()
    wide = jnp.concatenate(
        [
            jnp.concatenate([came[0:64, q * LANES:(q + 1) * LANES], came[64:128, q * LANES:(q + 1) * LANES]], axis=1)
            for q in range(NQ)
        ],
        axis=0,
    )
    done = dot3(wide, pair_hi, pair_lo)
    for q in range(NQ):
        for h in range(2):
            mixed[h * 64:(h + 1) * 64, q * LANES:(q + 1) * LANES] = done[
                q * 64:(q + 1) * 64, h * LANES:(h + 1) * LANES
            ]
    temper = mixed[:, 0:LANES]
    vapour = mixed[:, LANES:2 * LANES]
    condense = jnp.maximum(vapour - 0.5 * jnp.exp(0.3 * temper), 0.0)
    mixed[:, 0:LANES] = jnp.where(lane128 < HL, temper + 0.5 * condense, temper)
    mixed[:, LANES:2 * LANES] = jnp.where(lane128 < HL, vapour - condense, vapour)
    rate_ref[...] = jnp.where(lane < HL, condense[0:64], pltpu.roll(condense[64:128], HL, axis=1))
    hi, lo = split2(mixed[...])
    back[...] = dot(hi, perm_t[...]) + dot(lo, perm_t[...])

    def send_row(t, carry):
        dl, dz, dx, dy = lax.rem(t, 2), lax.rem(t // 2, 4), lax.rem(t // 8, 2), t // 16
        i = lax.rem(lax.rem(bx, 2) + dx, 2) * 32 + lax.rem(by + dy, 8) * 4 + lax.rem(bz + dz, 4)
        k = lax.rem(l + dl, 2)
        remote(row(back, k * 64 + i), row(home, b), back_send, back_recv, (s, l * 64 + i, k)).start()
        return carry

    lax.fori_loop(1, 128, send_row, 0, unroll=8)

    @pl.when(own)
    def _():
        pltpu.make_async_copy(row(back, slot), row(home, b), back_recv).start()
        pltpu.make_async_copy(row(back, slot), spare.at[1], back_send).start()

    @pl.when(jnp.logical_not(own))
    def _():
        send_row(0, 0)

    for h in range(2):
        rows_ref[:, h * CH:(h + 1) * CH] = back[h * 64:(h + 1) * 64, :]

    for k in range(2):
        remote(sst_out, sst_in.at[k], sst_send.at[k], sst_recv.at[k], (1 - s, b, k)).wait_recv()
    surface = sst_in[0] + sst_in[1]
    col = iota((8, LANES), 1)
    surface = jnp.where(col // NY == iota((8, LANES), 0), surface, 0.0)
    pick = jnp.where(lax.rem(iota((COLS, NY), 0), NY) == iota((COLS, NY), 1), F32(1), F32(0))
    sst_ref[...] = jnp.dot(surface, pick, precision=HIGH, preferred_element_type=F32)

    pltpu.make_async_copy(home, home, back_recv).wait()
    hi, lo = split2(home[...])
    adv_ref[...] = dot(hot_t, hi) + dot(hot_t, lo)

    pltpu.make_async_copy(gone, came, go_send).wait()
    pltpu.make_async_copy(back, home, back_send).wait()
    for c in sends:
        c.wait_send()
    for c in sst_copies:
        c.wait_send()


def on_device(
    state, u_wind, v_wind, mixing, stretch_order, remap_index, remap_weight, land_sea, ocean_temp, ocean_mixing,
):
    vmem = pl.BlockSpec(memory_space=pltpu.VMEM)
    dma = pltpu.SemaphoreType.DMA
    big = pltpu.VMEM((COLS, CH), F32)
    scratch = [
        pltpu.VMEM((CH, CH), BF16), pltpu.VMEM((CH, CH), BF16),
        pltpu.VMEM((COLS, LANES), F32), pltpu.VMEM((COLS, LANES), F32),
        big, big, big,
        pltpu.VMEM((NX, CH), F32), pltpu.VMEM((NX, CH), F32),
        pltpu.VMEM((2, NY, CH), F32), pltpu.VMEM((2, NY, CH), F32),
        pltpu.VMEM((2, NX, CH), F32),
        pltpu.VMEM((2, 1, CH), F32), pltpu.VMEM((2, 1, CH), F32),
        big, big,
        pltpu.VMEM((2, COLS, LANES), F32),
        pltpu.VMEM((8, LANES), F32), pltpu.VMEM((8, LANES), F32),
        pltpu.VMEM((8, LANES), F32), pltpu.VMEM((2, 8, LANES), F32),
        big, big, big,
        pltpu.VMEM((2, 1, CH), F32),
        dma((2, 5)), dma((2, 5)), dma, dma, dma, dma, dma((2,)), dma((2,)),
        dma, dma, dma, dma,
    ]
    outs = pl.pallas_call(
        window_kernel,
        out_shape=[
            jax.ShapeDtypeStruct((COLS, CH), F32),
            jax.ShapeDtypeStruct((64, LEV), F32),
            jax.ShapeDtypeStruct((64, LEV * NF), F32),
            jax.ShapeDtypeStruct(ocean_temp.shape, F32),
            jax.ShapeDtypeStruct((NX, NY), F32),
        ],
        in_specs=[vmem] * 10,
        out_specs=[vmem] * 5,
        scratch_shapes=scratch,
        compiler_params=pltpu.CompilerParams(
            collective_id=0, has_side_effects=True, vmem_limit_bytes=48 * 2**20
        ),
        name="window",
    )(
        state.reshape(COLS, CH),
        u_wind.reshape(COLS, HL),
        v_wind.reshape(COLS, HL),
        mixing,
        stretch_order.reshape(1, COLS),
        remap_index.T,
        remap_weight.T,
        land_sea.reshape(1, COLS),
        ocean_temp,
        ocean_mixing,
    )
    return (outs[0].reshape(state.shape), *outs[1:])


def solution(mesh):
    placed = (
        P("blk", "sec", "lev"),
        P("blk", "sec", "lev"),
        P("blk", "sec", "lev"),
        P(),
        P(("sec", "blk")),
        P(("sec", "blk", "lev"), None),
        P(("sec", "blk", "lev"), None),
        P(("sec", "blk", "lev")),
        P(None, ("sec", "blk", "lev")),
        P(),
    )
    return jax.shard_map(
        on_device,
        mesh=mesh,
        in_specs=placed,
        out_specs=(
            P("blk", "sec", "lev"),
            P(("sec", "blk", "lev"), None),
            P(("sec", "blk", "lev"), None),
            P(None, ("sec", "blk", "lev")),
            P("blk", "sec"),
        ),
        check_vma=False,
    )
```

time: 209 us -> 77.8 us (0.37)
  the two profiles are of different devices: /device:TPU:1 before, /device:TPU:5 now
where the time goes in v1:
time: 77.8 us; the launch traced here: 77.3 us
  Pallas kernels  67.6 us (87%)
  local copies, waits for them, and re-layouts  9.06 us (12%)
    pallas_call x1, Pallas kernels, on_device(): pl.pallas_call(window_kernel, out_shape=[jax.ShapeDtypeStruct((COLS, CH),...  67.6 us
    unnamed x25, local copies, waits for them, and re-layouts  9.06 us

profile of v1, /device:TPU:5, one launch (start us, length us, event | category | flops | bytes accessed | tf_op | source)
XLA Modules:
  0.0 77.3 jit_solution(1984173656093988995)
XLA Ops:
  0.6 0.0 copy-start.7
  0.6 0.0 copy-start.6
  0.7 0.0 copy-start.8
  0.7 0.0 copy-start.9
  0.7 0.6 copy-done.7
  1.3 0.0 copy-done.6
  1.3 0.0 copy-done.8
  1.3 0.0 copy-done.9
  1.3 0.0 copy-start
  1.3 1.0 %copy-done = f32[8,16,768]{2,1,0:T(8,128)S(1)} copy-done((f32[8,16,768]{2,1,0:T(8,128)S(1)}, f32[8,16,768]{2,1,0:T(8,128)}, u32[]{:S(2)}) %copy-start) | copy-done | bytes 393240
  2.3 0.0 copy-start.1
  2.3 0.8 %copy-done.1 = f32[8,16,64]{2,1,0:T(8,128)S(1)} copy-done((f32[8,16,64]{2,1,0:T(8,128)S(1)}, f32[8,16,64]{2,1,0:T(8,128)}, u32[]{:S(2)}) %copy-start.1) | copy-done | bytes 32792
  3.2 0.0 copy-start.2
  3.2 0.8 %copy-done.2 = f32[8,16,64]{2,1,0:T(8,128)S(1)} copy-done((f32[8,16,64]{2,1,0:T(8,128)S(1)}, f32[8,16,64]{2,1,0:T(8,128)}, u32[]{:S(2)}) %copy-start.2) | copy-done | bytes 32792
  4.0 0.0 copy-start.3
  4.0 0.8 %copy-done.3 = f32[128,128]{1,0:T(8,128)S(1)} copy-done((f32[128,128]{1,0:T(8,128)S(1)}, f32[128,128]{1,0:T(8,128)}, u32[]{:S(2)}) %copy-start.3) | copy-done | bytes 65560
  4.9 0.0 copy-start.4
  4.9 0.8 %copy-done.4 = f32[80,128]{1,0:T(8,128)S(1)} copy-done((f32[80,128]{1,0:T(8,128)S(1)}, f32[80,128]{1,0:T(8,128)}, u32[]{:S(2)}) %copy-start.4) | copy-done | bytes 40984
  5.6 0.0 copy-start.5
  5.6 0.8 %copy-done.5 = f32[80,80]{1,0:T(8,128)S(1)} copy-done((f32[80,80]{1,0:T(8,128)S(1)}, f32[80,80]{1,0:T(8,128)}, u32[]{:S(2)}) %copy-start.5) | copy-done | bytes 25624
  6.4 67.6 %window.1 = (f32[128,768]{1,0:T(8,128)S(1)}, f32[64,128]{1,0:T(8,128)S(1)}, f32[64,1536]{1,0:T(8,128)S(1)}, f32[80,128]{1,0:T(8,128)S(1)}, f32[8,16]{1,0:T(8,128)S(1)}) custom-call(f32[128,768]{1,0:T(8,128)S(1)} %bitcast.9, f32[128,64]{1,0:T(8,128)S(1)} %bitcast.10, f32[128,64]{1,0:T(8,128)S(1)} %bitcast.11, f32[128,128]{1,0:T(8,128)S(1)} %copy-done.3, ...), custom_call_target="tpu_custom_call" | custom-call | tf_op jit(solution)/shard_map/window/pallas_call | solution.py:381
  74.0 0.7 copy.20
  74.8 0.6 copy.21
  75.4 0.7 copy.22
  76.1 0.6 copy.23
  76.7 0.6 copy.24
Async XLA Ops:
  0.6 0.7 copy-start.7
  0.6 0.7 copy-start.6
  0.7 0.7 copy-start.8
  0.7 0.7 copy-start.9
  1.3 1.0 %copy-start = (f32[8,16,768]{2,1,0:T(8,128)S(1)}, f32[8,16,768]{2,1,0:T(8,128)}, u32[]{:S(2)}) copy-start(f32[8,16,768]{2,1,0:T(8,128)} %param.10) | copy-start | bytes 1179652
  2.3 0.8 %copy-start.1 = (f32[8,16,64]{2,1,0:T(8,128)S(1)}, f32[8,16,64]{2,1,0:T(8,128)}, u32[]{:S(2)}) copy-start(f32[8,16,64]{2,1,0:T(8,128)} %param.11) | copy-start | bytes 98308
  3.2 0.8 %copy-start.2 = (f32[8,16,64]{2,1,0:T(8,128)S(1)}, f32[8,16,64]{2,1,0:T(8,128)}, u32[]{:S(2)}) copy-start(f32[8,16,64]{2,1,0:T(8,128)} %param.12) | copy-start | bytes 98308
  4.0 0.8 %copy-start.3 = (f32[128,128]{1,0:T(8,128)S(1)}, f32[128,128]{1,0:T(8,128)}, u32[]{:S(2)}) copy-start(f32[128,128]{1,0:T(8,128)} %mixing_ref.1) | copy-start | bytes 196612
  4.9 0.8 %copy-start.4 = (f32[80,128]{1,0:T(8,128)S(1)}, f32[80,128]{1,0:T(8,128)}, u32[]{:S(2)}) copy-start(f32[80,128]{1,0:T(8,128)} %temp_ref.1) | copy-start | bytes 122884
  5.6 0.8 %copy-start.5 = (f32[80,80]{1,0:T(8,128)S(1)}, f32[80,80]{1,0:T(8,128)}, u32[]{:S(2)}) copy-start(f32[80,80]{1,0:T(8,128)} %omix_ref.1) | copy-start | bytes 76804

commit v2 on v1

--- a/solution.py
+++ b/solution.py
@@ -131,36 +131,45 @@
 
 
 def window_kernel(
+    state_hbm, u_hbm, v_hbm, mixing_hbm, order_hbm, index_hbm, weight_hbm, sea_hbm, temp_hbm, omix_hbm,
+    adv_hbm, rate_hbm, rows_hbm, curves_hbm, sst_hbm,
     state_ref, u_ref, v_ref, mixing_ref, order_ref, index_ref, weight_ref, sea_ref, temp_ref, omix_ref,
-    adv_ref, rate_ref, rows_ref, curves_ref, sst_ref,
+    adv_ref, rate_ref, rows_ref, curves_ref, sst_ref, in_sems, out_sems,
     perm, perm_t, uw, vw, field, adv1, adv2, edge1, edge2, xl, xr, ye, cl, cr,
     gone, came, tv, flux_out, flux_in, sst_out, sst_in, back, home, mixed, spare,
     halo_send, halo_recv, tv_send, tv_recv, flux_send, flux_recv, sst_send, sst_recv,
     go_send, go_recv, back_send, back_recv,
+    mid, mid2, plane, mid_send, mid_recv, stay_sem, home_send, home_recv, home_stay,
 ):
     s, b, l = lax.axis_index("sec"), lax.axis_index("blk"), lax.axis_index("lev")
     table = gll_derivative()
     left, right = lax.rem(b + NBLK - 1, NBLK), lax.rem(b + 1, NBLK)
-    half = b // 64
-    low = lax.rem(b, 64)
-    own = l == half
+
+    loads = [
+        pltpu.make_async_copy(src, dst, in_sems.at[i])
+        for i, (src, dst) in enumerate((
+            (state_hbm, state_ref), (u_hbm, u_ref), (v_hbm, v_ref), (order_hbm, order_ref), (mixing_hbm, mixing_ref),
+            (index_hbm, index_ref), (weight_hbm, weight_ref), (sea_hbm, sea_ref), (temp_hbm, temp_ref), (omix_hbm, omix_ref),
+        ))
+    ]
+    for c in loads:
+        c.start()
 
     barrier = pltpu.get_barrier_semaphore()
 
     def greet(device):
         pl.semaphore_signal(barrier, inc=1, device_id=device, device_id_type=MESH)
 
-    near = [(s, left, l), (s, right, l), (1 - s, b, l), (1 - s, left, l), (1 - s, right, l), (s, b, 1 - l), (1 - s, b, 1 - l)]
+    bx, by, bz = b // 32, lax.rem(b // 4, 8), lax.rem(b, 4)
+    pair = by // 2
+    along_x = [(s, lax.rem(bx + d, 4) * 32 + lax.rem(b, 32), l) for d in range(1, 4)]
+    along_y = [(s, bx * 32 + lax.rem(by + d, 8) * 4 + bz, l) for d in range(1, 8)]
+    along_z = [(s, bx * 32 + by * 4 + lax.rem(bz + d, 4), l) for d in range(1, 4)]
+    along_z += [(s, bx * 32 + by * 4 + lax.rem(bz + d, 4), 1 - l) for d in range(4)]
+    near = [(s, left, l), (s, right, l), (1 - s, b, l), (1 - s, left, l), (1 - s, right, l), (1 - s, b, 1 - l)]
+    near += along_x + along_z + along_y
     for device in near:
         greet(device)
-
-    def greet_sources(i, carry):
-        j = l * 64 + lax.rem(low + i, 64)
-        greet((s, j, 0))
-        greet((s, j, 1))
-        return carry
-
-    lax.fori_loop(0, 64, greet_sources, 0, unroll=8)
 
     for q in range(NQ):
         wide = (CH, LANES)
@@ -171,11 +180,16 @@
         perm_t[:, q * LANES:(q + 1) * LANES] = jnp.where(
             to == lax.rem(iota(wide, 0), HL) * NF + iota(wide, 0) // HL, F32(1), F32(0)
         ).astype(BF16)
+    for c in loads[:3]:
+        c.wait()
     hi, lo = split2(state_ref[...])
     field[...] = dot(hi, perm[...]) + dot(lo, perm[...])
     for ref, wind in ((uw, u_ref), (vw, v_ref)):
         w = F32(0.1) * wind[...]
         ref[...] = jnp.concatenate([w, w], axis=1)
+
+    for c in loads[3:]:
+        c.wait()
 
     square = (COLS, COLS)
     hot_t = jnp.where(iota(square, 0) == order_ref[...], F32(1), F32(0))
@@ -200,7 +214,9 @@
     calm = jnp.dot(omix_ref[...], temp_ref[...], precision=HIGH, preferred_element_type=F32)
 
     advect(field, uw, vw, adv1, table)
-    pl.semaphore_wait(barrier, len(near) + 128)
+    pl.semaphore_wait(barrier, len(near))
+    for device in along_y:
+        pl.semaphore_signal(plane, inc=1, device_id=device, device_id_type=MESH)
 
     sends = []
     for turn, (a, edge) in enumerate(((adv1, edge1), (adv2, edge2))):
@@ -228,6 +244,34 @@
         average(a, xl.at[turn], xr.at[turn], ye.at[turn], cl.at[turn], cr.at[turn], field, s)
 
     lane128 = iota((COLS, LANES), 1)
+    hi, lo = split2(field[...])
+    gone[...] = dot(hot, hi) + dot(hot, lo)
+    here = by * 4 + bz
+
+    def rows_of(turned):
+        return pl.ds(pl.multiple_of(turned * 8, 8), 8)
+
+    def block(x, turned):
+        return pl.ds(pl.multiple_of(x * 32 + turned * 8, 8), 8)
+
+    def in_pair(c, j):
+        y = lax.rem(pair + c, 4) * 2 + lax.rem(by + j // 8, 2)
+        return y * 4 + lax.rem(bz + j // 2, 4), lax.rem(l + j, 2)
+
+    across = []
+    for c in range(4):
+        turned = lax.rem(pair + c, 4)
+        for d in range(3):
+            copy = remote(
+                gone.at[block(lax.rem(bx + d + 1, 4), turned)], mid.at[bx, rows_of(turned)],
+                mid_send.at[c, d], mid_recv.at[c, d], along_x[d],
+            )
+            copy.start()
+            across.append(copy)
+    stay = pltpu.make_async_copy(gone.at[pl.ds(pl.multiple_of(bx * 32, 32), 32)], mid.at[bx], stay_sem)
+    stay.start()
+    sends += across
+
     tv[pl.ds(l, 1)] = jnp.where(
         lane128 < HL, field[:, 0:LANES], pltpu.roll(field[:, LANES:2 * LANES], HL, axis=1)
     )[None]
@@ -235,27 +279,66 @@
     tv_copy.start()
     sends.append(tv_copy)
 
-    hi, lo = split2(field[...])
-    gone[...] = dot(hot, hi) + dot(hot, lo)
-    slot = l * 64 + low
-    bx, by, bz = b // 32, lax.rem(b // 4, 8), lax.rem(b, 4)
-
-    def send_column(t, carry):
-        dz, dx, dy = lax.rem(t, 4), lax.rem(t // 4, 4), t // 16
-        p = lax.rem(bx + dx, 4) * 32 + lax.rem(by + dy, 8) * 4 + lax.rem(bz + dz, 4)
-        remote(row(gone, p), row(came, slot), go_send, go_recv, (s, p, half)).start()
-        return carry
-
-    lax.fori_loop(1, 128, send_column, 0, unroll=8)
-
-    @pl.when(own)
-    def _():
-        pltpu.make_async_copy(row(gone, b), row(came, slot), go_recv).start()
-        pltpu.make_async_copy(row(gone, b), spare.at[0], go_send).start()
-
-    @pl.when(jnp.logical_not(own))
-    def _():
-        send_column(0, 0)
+    pl.semaphore_wait(plane, len(along_y))
+    stay.wait()
+
+    def both_x(ref, h, place):
+        return ref.at[pl.ds(h * 2, 2), pl.ds(place, 1)]
+
+    for c in range(4):
+        for d in range(3):
+            across[c * 3 + d].wait_recv()
+
+        def send_columns(j, carry, c=c):
+            place, h = in_pair(c, j)
+            remote(
+                both_x(mid, h, place), both_x(came, l, here), go_send, go_recv, (s, bx * 32 + place, h)
+            ).start()
+            return carry
+
+        lax.fori_loop(1 if c == 0 else 0, 16, send_columns, 0, unroll=True)
+        if c == 0:
+            pltpu.make_async_copy(both_x(mid, l, here), both_x(came, l, here), go_recv).start()
+            pltpu.make_async_copy(both_x(mid, l, here), spare.at[0], go_send).start()
+
+    pltpu.make_async_copy(came, came, go_recv).wait()
+    wide = jnp.concatenate(
+        [
+            jnp.concatenate(
+                [came[h * 2:h * 2 + 2, :, q * LANES:(q + 1) * LANES].reshape(64, LANES) for h in range(2)], axis=1
+            )
+            for q in range(NQ)
+        ],
+        axis=0,
+    )
+    done = dot3(wide, pair_hi, pair_lo)
+    for q in range(NQ):
+        for h in range(2):
+            mixed[h * 64:(h + 1) * 64, q * LANES:(q + 1) * LANES] = done[
+                q * 64:(q + 1) * 64, h * LANES:(h + 1) * LANES
+            ]
+    temper = mixed[:, 0:LANES]
+    vapour = mixed[:, LANES:2 * LANES]
+    condense = jnp.maximum(vapour - 0.5 * jnp.exp(0.3 * temper), 0.0)
+    mixed[:, 0:LANES] = jnp.where(lane128 < HL, temper + 0.5 * condense, temper)
+    mixed[:, LANES:2 * LANES] = jnp.where(lane128 < HL, vapour - condense, vapour)
+    rate_ref[...] = jnp.where(lane < HL, condense[0:64], pltpu.roll(condense[64:128], HL, axis=1))
+    hi, lo = split2(mixed[...])
+    back[...] = (dot(hi, perm_t[...]) + dot(lo, perm_t[...])).reshape(4, 32, CH)
+
+    for c in range(4):
+
+        def send_rows(j, carry, c=c):
+            place, k = in_pair(c, j)
+            remote(
+                both_x(back, k, place), both_x(mid2, l, here), back_send, back_recv.at[c], (s, bx * 32 + place, k)
+            ).start()
+            return carry
+
+        lax.fori_loop(1 if c == 0 else 0, 16, send_rows, 0, unroll=True)
+        if c == 0:
+            pltpu.make_async_copy(both_x(back, l, here), both_x(mid2, l, here), back_recv.at[0]).start()
+            pltpu.make_async_copy(both_x(back, l, here), spare.at[1], back_send).start()
 
     tv_copy.wait_recv()
     whole = jnp.concatenate([tv[0], tv[1]], axis=1)
@@ -276,6 +359,25 @@
     flux_copy.start()
     sends.append(flux_copy)
 
+    def pass_rows(c):
+        turned = lax.rem(pair + 4 - c, 4)
+        arrived = mid2.at[:, rows_of(turned)]
+        pltpu.make_async_copy(arrived, arrived, back_recv.at[c]).wait()
+        for d in range(3):
+            copy = remote(
+                mid2.at[lax.rem(bx + d + 1, 4), rows_of(turned)], home.at[block(bx, turned)],
+                home_send.at[c, d], home_recv.at[c, d], along_x[d],
+            )
+            copy.start()
+            last.append(copy)
+        copy = pltpu.make_async_copy(mid2.at[bx, rows_of(turned)], home.at[block(bx, turned)], home_stay.at[c])
+        copy.start()
+        stays.append(copy)
+
+    last, stays = [], []
+    pass_rows(0)
+    pass_rows(1)
+
     flux_copy.wait_recv()
     forcing = jnp.dot(flux_in[...], weigh, precision=HIGH, preferred_element_type=F32)
     forcing = sea * forcing[0:1]
@@ -291,49 +393,27 @@
     for c in sst_copies:
         c.start()
 
-    pltpu.make_async_copy(came, came, go_recv).wait()
-    wide = jnp.concatenate(
-        [
-            jnp.concatenate([came[0:64, q * LANES:(q + 1) * LANES], came[64:128, q * LANES:(q + 1) * LANES]], axis=1)
-            for q in range(NQ)
-        ],
-        axis=0,
-    )
-    done = dot3(wide, pair_hi, pair_lo)
-    for q in range(NQ):
-        for h in range(2):
-            mixed[h * 64:(h + 1) * 64, q * LANES:(q + 1) * LANES] = done[
-                q * 64:(q + 1) * 64, h * LANES:(h + 1) * LANES
-            ]
-    temper = mixed[:, 0:LANES]
-    vapour = mixed[:, LANES:2 * LANES]
-    condense = jnp.maximum(vapour - 0.5 * jnp.exp(0.3 * temper), 0.0)
-    mixed[:, 0:LANES] = jnp.where(lane128 < HL, temper + 0.5 * condense, temper)
-    mixed[:, LANES:2 * LANES] = jnp.where(lane128 < HL, vapour - condense, vapour)
-    rate_ref[...] = jnp.where(lane < HL, condense[0:64], pltpu.roll(condense[64:128], HL, axis=1))
-    hi, lo = split2(mixed[...])
-    back[...] = dot(hi, perm_t[...]) + dot(lo, perm_t[...])
-
-    def send_row(t, carry):
-        dl, dz, dx, dy = lax.rem(t, 2), lax.rem(t // 2, 4), lax.rem(t // 8, 2), t // 16
-        i = lax.rem(lax.rem(bx, 2) + dx, 2) * 32 + lax.rem(by + dy, 8) * 4 + lax.rem(bz + dz, 4)
-        k = lax.rem(l + dl, 2)
-        remote(row(back, k * 64 + i), row(home, b), back_send, back_recv, (s, l * 64 + i, k)).start()
-        return carry
-
-    lax.fori_loop(1, 128, send_row, 0, unroll=8)
-
-    @pl.when(own)
-    def _():
-        pltpu.make_async_copy(row(back, slot), row(home, b), back_recv).start()
-        pltpu.make_async_copy(row(back, slot), spare.at[1], back_send).start()
-
-    @pl.when(jnp.logical_not(own))
-    def _():
-        send_row(0, 0)
-
+    pass_rows(2)
+    pass_rows(3)
     for h in range(2):
-        rows_ref[:, h * CH:(h + 1) * CH] = back[h * 64:(h + 1) * 64, :]
+        rows_ref[:, h * CH:(h + 1) * CH] = back[h * 2:h * 2 + 2].reshape(64, CH)
+
+    def store(i, src, dst):
+        c = pltpu.make_async_copy(src, dst, out_sems.at[i])
+        c.start()
+        return c
+
+    stores = [store(0, rate_ref, rate_hbm), store(1, rows_ref, rows_hbm), store(2, curves_ref, curves_hbm)]
+
+    for c in stays:
+        c.wait()
+    for c in last:
+        c.wait_recv()
+    sends += last
+    hi, lo = split2(home[...])
+    adv_ref[...] = dot(hot_t, hi) + dot(hot_t, lo)
+
+    stores.append(store(3, adv_ref, adv_hbm))
 
     for k in range(2):
         remote(sst_out, sst_in.at[k], sst_send.at[k], sst_recv.at[k], (1 - s, b, k)).wait_recv()
@@ -343,24 +423,37 @@
     pick = jnp.where(lax.rem(iota((COLS, NY), 0), NY) == iota((COLS, NY), 1), F32(1), F32(0))
     sst_ref[...] = jnp.dot(surface, pick, precision=HIGH, preferred_element_type=F32)
 
-    pltpu.make_async_copy(home, home, back_recv).wait()
-    hi, lo = split2(home[...])
-    adv_ref[...] = dot(hot_t, hi) + dot(hot_t, lo)
-
-    pltpu.make_async_copy(gone, came, go_send).wait()
-    pltpu.make_async_copy(back, home, back_send).wait()
+    stores.append(store(4, sst_ref, sst_hbm))
+    pltpu.make_async_copy(mid, came, go_send).wait()
+    pltpu.make_async_copy(back, mid2, back_send).wait()
     for c in sends:
         c.wait_send()
     for c in sst_copies:
         c.wait_send()
+    for c in stores:
+        c.wait()
+
+
+def hand_over(*refs):
+    src, dst, held, sems = refs[:5], refs[5:10], refs[10:15], refs[15]
+    loads = [pltpu.make_async_copy(src[i], held[i], sems.at[0, i]) for i in range(5)]
+    stores = [pltpu.make_async_copy(held[i], dst[i], sems.at[1, i]) for i in range(5)]
+    for c in loads:
+        c.start()
+    for a, b in zip(loads, stores):
+        a.wait()
+        b.start()
+    for c in stores:
+        c.wait()
 
 
 def on_device(
     state, u_wind, v_wind, mixing, stretch_order, remap_index, remap_weight, land_sea, ocean_temp, ocean_mixing,
 ):
-    vmem = pl.BlockSpec(memory_space=pltpu.VMEM)
+    hbm = pl.BlockSpec(memory_space=pltpu.HBM)
     dma = pltpu.SemaphoreType.DMA
     big = pltpu.VMEM((COLS, CH), F32)
+    split = pltpu.VMEM((4, 32, CH), F32)
     scratch = [
         pltpu.VMEM((CH, CH), BF16), pltpu.VMEM((CH, CH), BF16),
         pltpu.VMEM((COLS, LANES), F32), pltpu.VMEM((COLS, LANES), F32),
@@ -369,32 +462,25 @@
         pltpu.VMEM((2, NY, CH), F32), pltpu.VMEM((2, NY, CH), F32),
         pltpu.VMEM((2, NX, CH), F32),
         pltpu.VMEM((2, 1, CH), F32), pltpu.VMEM((2, 1, CH), F32),
-        big, big,
+        big, split,
         pltpu.VMEM((2, COLS, LANES), F32),
         pltpu.VMEM((8, LANES), F32), pltpu.VMEM((8, LANES), F32),
         pltpu.VMEM((8, LANES), F32), pltpu.VMEM((2, 8, LANES), F32),
-        big, big, big,
-        pltpu.VMEM((2, 1, CH), F32),
+        split, big, big,
+        pltpu.VMEM((2, 2, 1, CH), F32),
         dma((2, 5)), dma((2, 5)), dma, dma, dma, dma, dma((2,)), dma((2,)),
-        dma, dma, dma, dma,
+        dma, dma, dma, dma((4,)),
+        split, split, pltpu.SemaphoreType.REGULAR,
+        dma((4, 3)), dma((4, 3)), dma, dma((4, 3)), dma((4, 3)), dma((4,)),
     ]
-    outs = pl.pallas_call(
-        window_kernel,
-        out_shape=[
+    out_shape = [
             jax.ShapeDtypeStruct((COLS, CH), F32),
             jax.ShapeDtypeStruct((64, LEV), F32),
             jax.ShapeDtypeStruct((64, LEV * NF), F32),
             jax.ShapeDtypeStruct(ocean_temp.shape, F32),
             jax.ShapeDtypeStruct((NX, NY), F32),
-        ],
-        in_specs=[vmem] * 10,
-        out_specs=[vmem] * 5,
-        scratch_shapes=scratch,
-        compiler_params=pltpu.CompilerParams(
-            collective_id=0, has_side_effects=True, vmem_limit_bytes=48 * 2**20
-        ),
-        name="window",
-    )(
+    ]
+    ins = (
         state.reshape(COLS, CH),
         u_wind.reshape(COLS, HL),
         v_wind.reshape(COLS, HL),
@@ -406,6 +492,27 @@
         ocean_temp,
         ocean_mixing,
     )
+    held = [pltpu.VMEM(a.shape, a.dtype) for a in (*ins, *out_shape)]
+    outs = pl.pallas_call(
+        window_kernel,
+        out_shape=out_shape,
+        in_specs=[hbm] * 10,
+        out_specs=[hbm] * 5,
+        scratch_shapes=[*held, dma((10,)), dma((5,)), *scratch],
+        compiler_params=pltpu.CompilerParams(
+            collective_id=0, has_side_effects=True, vmem_limit_bytes=56 * 2**20
+        ),
+        name="window",
+    )(*ins)
+    outs = pl.pallas_call(
+        hand_over,
+        out_shape=out_shape,
+        in_specs=[hbm] * 5,
+        out_specs=[hbm] * 5,
+        scratch_shapes=[*(pltpu.VMEM(a.shape, a.dtype) for a in out_shape), dma((2, 5))],
+        compiler_params=pltpu.CompilerParams(vmem_limit_bytes=56 * 2**20),
+        name="outputs",
+    )(*outs)
     return (outs[0].reshape(state.shape), *outs[1:])
 
 

time: 77.8 us -> 66.2 us (0.85)
  the two profiles are of different devices: /device:TPU:5 before, /device:TPU:1 now
where the time goes in v2:
time: 66.2 us; the launch traced here: 65.3 us
  Pallas kernels  64.7 us (98%)
    pallas_call x1, Pallas kernels, on_device(): pl.pallas_call(window_kernel, out_shape=out_shape, in_specs=[hbm] * 10, o...  62.7 us
    pallas_call x1, Pallas kernels, on_device(): pl.pallas_call(hand_over, out_shape=out_shape, in_specs=[hbm] * 5, out_sp...  1.97 us

profile of v2, /device:TPU:1, one launch (start us, length us, event | category | flops | bytes accessed | tf_op | source)
XLA Modules:
  0.0 65.3 jit_solution(13267403010670255645)
XLA Ops:
  0.6 62.7 %window.1 = (f32[128,768]{1,0:T(8,128)}, f32[64,128]{1,0:T(8,128)}, f32[64,1536]{1,0:T(8,128)}, f32[80,128]{1,0:T(8,128)}, f32[8,16]{1,0:T(8,128)}) custom-call(f32[128,768]{1,0:T(8,128)} %bitcast.8, f32[128,64]{1,0:T(8,128)} %bitcast.9, f32[128,64]{1,0:T(8,128)} %bitcast.10, f32[128,128]{1,0:T(8,128)} %mixing_hbm.1, s32[1,128]{1,0:T(1,128)} %bitcast.13, ...), custom_call_target="tpu_custom_call" | custom-call | tf_op jit(solution)/shard_map/window/pallas_call | solution.py:496
  63.4 2.0 %outputs.1 = (f32[128,768]{1,0:T(8,128)}, f32[64,128]{1,0:T(8,128)}, f32[64,1536]{1,0:T(8,128)}, f32[80,128]{1,0:T(8,128)}, f32[8,16]{1,0:T(8,128)}) custom-call(f32[128,768]{1,0:T(8,128)} %get-tuple-element.15.refs_0_, f32[64,128]{1,0:T(8,128)} %get-tuple-element.16.refs_1_, f32[64,1536]{1,0:T(8,128)} %get-tuple-element.17.refs_2_, ...), custom_call_target="tpu_custom_call" | custom-call | tf_op jit(solution)/shard_map/outputs/pallas_call | solution.py:507

commit v3 on v2

--- a/solution.py
+++ b/solution.py
@@ -72,7 +72,7 @@
     return ref.at[pl.ds(r, 1)]
 
 
-def advect(field_ref, uw_ref, vw_ref, out_ref, table):
+def advect(field_ref, uw_ref, vw_ref, out_ref, table, part):
     y8 = iota((8, LANES), 0)
     at = lax.rem(y8, NP)
     coefs = {}
@@ -82,7 +82,7 @@
             if 0 <= i + d < NP:
                 c = jnp.where(at == i, F32(table[i, i + d]), c)
         coefs[d] = c[None]
-    for q in range(NQ):
+    for q in range(part * 3, part * 3 + 3):
         lanes = slice(q * LANES, (q + 1) * LANES)
         for e in range(2):
             rows = slice(e * 64, (e + 1) * 64)
@@ -104,13 +104,13 @@
             )
 
 
-def average(a_ref, x_from_left, x_from_right, edge_ref, cor_l, cor_r, out_ref, s):
+def average(a_ref, x_from_left, x_from_right, edge_ref, cor_l, cor_r, out_ref, s, part):
     y = iota((NY, LANES), 0)
     i = lax.rem(y, NP)
     at_edge = ((y == NY - 1) & (s == 0)) | ((y == 0) & (s == 1))
     closed = ((y == NY - 1) & (s == 1)) | ((y == 0) & (s == 0))
     inside = ((i == 0) | (i == NP - 1)) & jnp.logical_not(closed)
-    for q in range(NQ):
+    for q in range(part * 3, part * 3 + 3):
         lanes = slice(q * LANES, (q + 1) * LANES)
         a = [a_ref[x * NY:(x + 1) * NY, lanes] for x in range(NX)]
         e = edge_ref[:, lanes]
@@ -213,39 +213,50 @@
         weigh = weigh + jnp.where(iota(square, 0) == index_ref[m:m + 1, :], weight_ref[m:m + 1, :], F32(0))
     calm = jnp.dot(omix_ref[...], temp_ref[...], precision=HIGH, preferred_element_type=F32)
 
-    advect(field, uw, vw, adv1, table)
-    pl.semaphore_wait(barrier, len(near))
-    for device in along_y:
-        pl.semaphore_signal(plane, inc=1, device_id=device, device_id_type=MESH)
-
     sends = []
-    for turn, (a, edge) in enumerate(((adv1, edge1), (adv2, edge2))):
-        if turn == 1:
-            advect(field, uw, vw, a, table)
+
+    def exchange(turn, part):
+        a, edge = ((adv1, edge1), (adv2, edge2))[turn]
+        lanes = slice(part * CH // 2, (part + 1) * CH // 2)
+        cut = pl.ds(part * CH // 2, CH // 2)
         for x in range(NX):
-            bottom, top = a[x * NY:x * NY + 1, :], a[(x + 1) * NY - 1:(x + 1) * NY, :]
-            edge[x:x + 1, :] = jnp.where(s == 0, top, bottom)
+            bottom, top = a[x * NY:x * NY + 1, lanes], a[(x + 1) * NY - 1:(x + 1) * NY, lanes]
+            edge[x:x + 1, lanes] = jnp.where(s == 0, top, bottom)
         parts = (
-            (a.at[pl.ds(0, NY)], xr.at[turn], (s, left, l)),
-            (a.at[pl.ds(COLS - NY, NY)], xl.at[turn], (s, right, l)),
-            (edge, ye.at[turn], (1 - s, b, l)),
-            (row(edge, 0), cr.at[turn], (1 - s, left, l)),
-            (row(edge, NX - 1), cl.at[turn], (1 - s, right, l)),
+            (a.at[pl.ds(0, NY), cut], xr.at[turn, :, cut], (s, left, l)),
+            (a.at[pl.ds(COLS - NY, NY), cut], xl.at[turn, :, cut], (s, right, l)),
+            (edge.at[:, cut], ye.at[turn, :, cut], (1 - s, b, l)),
+            (edge.at[pl.ds(0, 1), cut], cr.at[turn, :, cut], (1 - s, left, l)),
+            (edge.at[pl.ds(NX - 1, 1), cut], cl.at[turn, :, cut], (1 - s, right, l)),
         )
         copies = [
-            remote(src, dst, halo_send.at[turn, i], halo_recv.at[turn, i], device)
+            remote(src, dst, halo_send.at[turn, part, i], halo_recv.at[turn, part, i], device)
             for i, (src, dst, device) in enumerate(parts)
         ]
         for c in copies:
             c.start()
+        sends.extend(copies)
+        return copies
+
+    def settle(turn, part, copies):
         for c in copies:
             c.wait_recv()
-        sends += copies
-        average(a, xl.at[turn], xr.at[turn], ye.at[turn], cl.at[turn], cr.at[turn], field, s)
+        a = (adv1, adv2)[turn]
+        average(a, xl.at[turn], xr.at[turn], ye.at[turn], cl.at[turn], cr.at[turn], field, s, part)
+
+    for part in range(2):
+        advect(field, uw, vw, adv1, table, part)
+    pl.semaphore_wait(barrier, len(near))
+    first = [exchange(0, part) for part in range(2)]
+    for device in along_y:
+        pl.semaphore_signal(plane, inc=1, device_id=device, device_id_type=MESH)
+    second = []
+    for part in range(2):
+        settle(0, part, first[part])
+        advect(field, uw, vw, adv2, table, part)
+        second.append(exchange(1, part))
 
     lane128 = iota((COLS, LANES), 1)
-    hi, lo = split2(field[...])
-    gone[...] = dot(hot, hi) + dot(hot, lo)
     here = by * 4 + bz
 
     def rows_of(turned):
@@ -259,25 +270,31 @@
         return y * 4 + lax.rem(bz + j // 2, 4), lax.rem(l + j, 2)
 
     across = []
-    for c in range(4):
-        turned = lax.rem(pair + c, 4)
-        for d in range(3):
-            copy = remote(
-                gone.at[block(lax.rem(bx + d + 1, 4), turned)], mid.at[bx, rows_of(turned)],
-                mid_send.at[c, d], mid_recv.at[c, d], along_x[d],
-            )
-            copy.start()
-            across.append(copy)
+    for part in range(2):
+        settle(1, part, second[part])
+        if part == 0:
+            tv[pl.ds(l, 1)] = jnp.where(
+                lane128 < HL, field[:, 0:LANES], pltpu.roll(field[:, LANES:2 * LANES], HL, axis=1)
+            )[None]
+            tv_copy = remote(tv.at[l], tv.at[l], tv_send, tv_recv, (s, b, 1 - l))
+            tv_copy.start()
+            sends.append(tv_copy)
+        lanes = slice(part * CH // 2, (part + 1) * CH // 2)
+        cut = pl.ds(part * CH // 2, CH // 2)
+        hi, lo = split2(field[:, lanes])
+        gone[:, lanes] = dot(hot, hi) + dot(hot, lo)
+        for c in range(4):
+            turned = lax.rem(pair + c, 4)
+            for d in range(3):
+                copy = remote(
+                    gone.at[block(lax.rem(bx + d + 1, 4), turned), cut], mid.at[bx, rows_of(turned), cut],
+                    mid_send.at[c, d, part], mid_recv.at[c, d, part], along_x[d],
+                )
+                copy.start()
+                across.append((c, copy))
+                sends.append(copy)
     stay = pltpu.make_async_copy(gone.at[pl.ds(pl.multiple_of(bx * 32, 32), 32)], mid.at[bx], stay_sem)
     stay.start()
-    sends += across
-
-    tv[pl.ds(l, 1)] = jnp.where(
-        lane128 < HL, field[:, 0:LANES], pltpu.roll(field[:, LANES:2 * LANES], HL, axis=1)
-    )[None]
-    tv_copy = remote(tv.at[l], tv.at[l], tv_send, tv_recv, (s, b, 1 - l))
-    tv_copy.start()
-    sends.append(tv_copy)
 
     pl.semaphore_wait(plane, len(along_y))
     stay.wait()
@@ -286,59 +303,80 @@
         return ref.at[pl.ds(h * 2, 2), pl.ds(place, 1)]
 
     for c in range(4):
-        for d in range(3):
-            across[c * 3 + d].wait_recv()
+        for k, copy in across:
+            if k == c:
+                copy.wait_recv()
 
         def send_columns(j, carry, c=c):
             place, h = in_pair(c, j)
             remote(
-                both_x(mid, h, place), both_x(came, l, here), go_send, go_recv, (s, bx * 32 + place, h)
+                both_x(mid, h, place), both_x(came, l, here), go_send, go_recv.at[c], (s, bx * 32 + place, h)
             ).start()
             return carry
 
         lax.fori_loop(1 if c == 0 else 0, 16, send_columns, 0, unroll=True)
         if c == 0:
-            pltpu.make_async_copy(both_x(mid, l, here), both_x(came, l, here), go_recv).start()
+            pltpu.make_async_copy(both_x(mid, l, here), both_x(came, l, here), go_recv.at[0]).start()
             pltpu.make_async_copy(both_x(mid, l, here), spare.at[0], go_send).start()
 
-    pltpu.make_async_copy(came, came, go_recv).wait()
-    wide = jnp.concatenate(
-        [
-            jnp.concatenate(
-                [came[h * 2:h * 2 + 2, :, q * LANES:(q + 1) * LANES].reshape(64, LANES) for h in range(2)], axis=1
-            )
-            for q in range(NQ)
-        ],
-        axis=0,
-    )
-    done = dot3(wide, pair_hi, pair_lo)
-    for q in range(NQ):
-        for h in range(2):
-            mixed[h * 64:(h + 1) * 64, q * LANES:(q + 1) * LANES] = done[
-                q * 64:(q + 1) * 64, h * LANES:(h + 1) * LANES
-            ]
-    temper = mixed[:, 0:LANES]
-    vapour = mixed[:, LANES:2 * LANES]
-    condense = jnp.maximum(vapour - 0.5 * jnp.exp(0.3 * temper), 0.0)
-    mixed[:, 0:LANES] = jnp.where(lane128 < HL, temper + 0.5 * condense, temper)
-    mixed[:, LANES:2 * LANES] = jnp.where(lane128 < HL, vapour - condense, vapour)
-    rate_ref[...] = jnp.where(lane < HL, condense[0:64], pltpu.roll(condense[64:128], HL, axis=1))
-    hi, lo = split2(mixed[...])
-    back[...] = (dot(hi, perm_t[...]) + dot(lo, perm_t[...])).reshape(4, 32, CH)
-
-    for c in range(4):
-
-        def send_rows(j, carry, c=c):
-            place, k = in_pair(c, j)
-            remote(
-                both_x(back, k, place), both_x(mid2, l, here), back_send, back_recv.at[c], (s, bx * 32 + place, k)
-            ).start()
-            return carry
-
-        lax.fori_loop(1 if c == 0 else 0, 16, send_rows, 0, unroll=True)
-        if c == 0:
-            pltpu.make_async_copy(both_x(back, l, here), both_x(mid2, l, here), back_recv.at[0]).start()
-            pltpu.make_async_copy(both_x(back, l, here), spare.at[1], back_send).start()
+    lane64 = iota((64, LANES), 1)
+    for step in range(2):
+        turns = []
+        for c in (step * 2, step * 2 + 1):
+            turns.append(lax.rem(pair + 4 - c, 4))
+            arrived = came.at[:, rows_of(turns[-1])]
+            pltpu.make_async_copy(arrived, arrived, go_recv.at[c]).wait()
+        loaded = [came[:, rows_of(t), :] for t in turns]
+        wide = jnp.concatenate(
+            [
+                jnp.concatenate(
+                    [
+                        jnp.concatenate(
+                            [a[h * 2:h * 2 + 2, :, q * LANES:(q + 1) * LANES].reshape(16, LANES) for a in loaded], axis=0
+                        )
+                        for h in range(2)
+                    ],
+                    axis=1,
+                )
+                for q in range(NQ)
+            ],
+            axis=0,
+        )
+        done = dot3(wide, pair_hi, pair_lo)
+        for q in range(NQ):
+            for h in range(2):
+                mixed[h * 32:(h + 1) * 32, q * LANES:(q + 1) * LANES] = done[
+                    q * 32:(q + 1) * 32, h * LANES:(h + 1) * LANES
+                ]
+        temper = mixed[:, 0:LANES]
+        vapour = mixed[:, LANES:2 * LANES]
+        condense = jnp.maximum(vapour - 0.5 * jnp.exp(0.3 * temper), 0.0)
+        mixed[:, 0:LANES] = jnp.where(lane64 < HL, temper + 0.5 * condense, temper)
+        mixed[:, LANES:2 * LANES] = jnp.where(lane64 < HL, vapour - condense, vapour)
+        hi, lo = split2(mixed[...])
+        ready = dot(hi, perm_t[...]) + dot(lo, perm_t[...])
+        for n, t in enumerate(turns):
+            for h in range(2):
+                for x in range(2):
+                    at = h * 32 + n * 16 + x * 8
+                    back[h * 2 + x, rows_of(t), :] = ready[at:at + 8]
+        rate = jnp.where(lane64[0:32] < HL, condense[0:32], pltpu.roll(condense[32:64], HL, axis=1))
+        for n, t in enumerate(turns):
+            for x in range(2):
+                rate_ref[block(x, t), :] = rate[n * 16 + x * 8:n * 16 + x * 8 + 8]
+        for c in (step * 2, step * 2 + 1):
+
+            def send_rows(j, carry, c=c):
+                place, k = in_pair((4 - c) % 4, j)
+                remote(
+                    both_x(back, k, place), both_x(mid2, l, here), back_send, back_recv.at[c], (s, bx * 32 + place, k)
+                ).start()
+                return carry
+
+            lax.fori_loop(1 if c == 0 else 0, 16, send_rows, 0, unroll=True)
+            if c == 0:
+                pltpu.make_async_copy(both_x(back, l, here), both_x(mid2, l, here), back_recv.at[0]).start()
+                pltpu.make_async_copy(both_x(back, l, here), spare.at[1], back_send).start()
 
     tv_copy.wait_recv()
     whole = jnp.concatenate([tv[0], tv[1]], axis=1)
@@ -360,7 +398,7 @@
     sends.append(flux_copy)
 
     def pass_rows(c):
-        turned = lax.rem(pair + 4 - c, 4)
+        turned = lax.rem(pair + c, 4)
         arrived = mid2.at[:, rows_of(turned)]
         pltpu.make_async_copy(arrived, arrived, back_recv.at[c]).wait()
         for d in range(3):
@@ -405,6 +443,16 @@
 
     stores = [store(0, rate_ref, rate_hbm), store(1, rows_ref, rows_hbm), store(2, curves_ref, curves_hbm)]
 
+    for k in range(2):
+        remote(sst_out, sst_in.at[k], sst_send.at[k], sst_recv.at[k], (1 - s, b, k)).wait_recv()
+    surface = sst_in[0] + sst_in[1]
+    col = iota((8, LANES), 1)
+    surface = jnp.where(col // NY == iota((8, LANES), 0), surface, 0.0)
+    pick = jnp.where(lax.rem(iota((COLS, NY), 0), NY) == iota((COLS, NY), 1), F32(1), F32(0))
+    sst_ref[...] = jnp.dot(surface, pick, precision=HIGH, preferred_element_type=F32)
+
+    stores.append(store(4, sst_ref, sst_hbm))
+
     for c in stays:
         c.wait()
     for c in last:
@@ -415,15 +463,6 @@
 
     stores.append(store(3, adv_ref, adv_hbm))
 
-    for k in range(2):
-        remote(sst_out, sst_in.at[k], sst_send.at[k], sst_recv.at[k], (1 - s, b, k)).wait_recv()
-    surface = sst_in[0] + sst_in[1]
-    col = iota((8, LANES), 1)
-    surface = jnp.where(col // NY == iota((8, LANES), 0), surface, 0.0)
-    pick = jnp.where(lax.rem(iota((COLS, NY), 0), NY) == iota((COLS, NY), 1), F32(1), F32(0))
-    sst_ref[...] = jnp.dot(surface, pick, precision=HIGH, preferred_element_type=F32)
-
-    stores.append(store(4, sst_ref, sst_hbm))
     pltpu.make_async_copy(mid, came, go_send).wait()
     pltpu.make_async_copy(back, mid2, back_send).wait()
     for c in sends:
@@ -466,12 +505,12 @@
         pltpu.VMEM((2, COLS, LANES), F32),
         pltpu.VMEM((8, LANES), F32), pltpu.VMEM((8, LANES), F32),
         pltpu.VMEM((8, LANES), F32), pltpu.VMEM((2, 8, LANES), F32),
-        split, big, big,
+        split, big, pltpu.VMEM((64, CH), F32),
         pltpu.VMEM((2, 2, 1, CH), F32),
-        dma((2, 5)), dma((2, 5)), dma, dma, dma, dma, dma((2,)), dma((2,)),
-        dma, dma, dma, dma((4,)),
+        dma((2, 2, 5)), dma((2, 2, 5)), dma, dma, dma, dma, dma((2,)), dma((2,)),
+        dma, dma((4,)), dma, dma((4,)),
         split, split, pltpu.SemaphoreType.REGULAR,
-        dma((4, 3)), dma((4, 3)), dma, dma((4, 3)), dma((4, 3)), dma((4,)),
+        dma((4, 3, 2)), dma((4, 3, 2)), dma, dma((4, 3)), dma((4, 3)), dma((4,)),
     ]
     out_shape = [
             jax.ShapeDtypeStruct((COLS, CH), F32),

time: 66.2 us -> 63.4 us (0.958); the launches traced: 65.3 us -> 63.2 us
  Pallas kernels: 64.7 us -> 62.6 us
    pallas_call x1, Pallas kernels: 62.7 us -> 60.6 us  [on_device(): pl.pallas_call(window_kernel, out_shape=out_shape, in_specs=[hbm] * 10, o...]
where the time goes in v3:
time: 63.4 us; the launch traced here: 63.2 us
  Pallas kernels  62.6 us (99%)
  between operations  0.64 us (1%)
    pallas_call x1, Pallas kernels, on_device(): pl.pallas_call(window_kernel, out_shape=out_shape, in_specs=[hbm] * 10, o...  60.6 us
    pallas_call x1, Pallas kernels, on_device(): pl.pallas_call(hand_over, out_shape=out_shape, in_specs=[hbm] * 5, out_sp...  1.97 us

profile of v3, /device:TPU:1, one launch (start us, length us, event | category | flops | bytes accessed | tf_op | source)
XLA Modules:
  0.0 63.2 jit_solution(9910974219074459076)
XLA Ops:
  0.6 60.6 %window.1 = (f32[128,768]{1,0:T(8,128)}, f32[64,128]{1,0:T(8,128)}, f32[64,1536]{1,0:T(8,128)}, f32[80,128]{1,0:T(8,128)}, f32[8,16]{1,0:T(8,128)}) custom-call(f32[128,768]{1,0:T(8,128)} %bitcast.8, f32[128,64]{1,0:T(8,128)} %bitcast.9, f32[128,64]{1,0:T(8,128)} %bitcast.10, f32[128,128]{1,0:T(8,128)} %mixing_hbm.1, s32[1,128]{1,0:T(1,128)} %bitcast.13, ...), custom_call_target="tpu_custom_call" | custom-call | tf_op jit(solution)/shard_map/window/pallas_call | solution.py:535
  61.2 2.0 %outputs.1 = (f32[128,768]{1,0:T(8,128)}, f32[64,128]{1,0:T(8,128)}, f32[64,1536]{1,0:T(8,128)}, f32[80,128]{1,0:T(8,128)}, f32[8,16]{1,0:T(8,128)}) custom-call(f32[128,768]{1,0:T(8,128)} %get-tuple-element.15.refs_0_, f32[64,128]{1,0:T(8,128)} %get-tuple-element.16.refs_1_, f32[64,1536]{1,0:T(8,128)} %get-tuple-element.17.refs_2_, ...), custom_call_target="tpu_custom_call" | custom-call | tf_op jit(solution)/shard_map/outputs/pallas_call | solution.py:546

commit v4 on v3

--- a/solution.py
+++ b/solution.py
@@ -19,6 +19,7 @@
 NBLK = 128
 LANES = 128
 NQ = CH // LANES
+PAIRS = (2, 0, 1, 3)
 F32 = jnp.float32
 BF16 = jnp.bfloat16
 HIGH = lax.Precision.HIGHEST
@@ -58,7 +59,17 @@
 
 def dot3(a, b_hi, b_lo):
     hi, lo = split2(a)
-    return dot(hi, b_hi) + dot(lo, b_hi) + dot(hi, b_lo)
+    both = dot(jnp.concatenate([hi, lo], axis=0), b_hi)
+    return both[:a.shape[0]] + both[a.shape[0]:] + dot(hi, b_lo)
+
+
+def dot_rows(a, hot):
+    both = dot(jnp.concatenate(split2(a), axis=0), hot)
+    return both[:a.shape[0]] + both[a.shape[0]:]
+
+
+def pick_rows(hot, a):
+    return dot(jnp.concatenate([hot, hot], axis=1), jnp.concatenate(split2(a), axis=0))
 
 
 def remote(src, dst, send, recv, device):
@@ -132,11 +143,11 @@
 
 def window_kernel(
     state_hbm, u_hbm, v_hbm, mixing_hbm, order_hbm, index_hbm, weight_hbm, sea_hbm, temp_hbm, omix_hbm,
-    adv_hbm, rate_hbm, rows_hbm, curves_hbm, sst_hbm,
+    home, rate_hbm, rows_hbm, curves_hbm, sst_hbm,
     state_ref, u_ref, v_ref, mixing_ref, order_ref, index_ref, weight_ref, sea_ref, temp_ref, omix_ref,
-    adv_ref, rate_ref, rows_ref, curves_ref, sst_ref, in_sems, out_sems,
+    rate_ref, rows_ref, curves_ref, sst_ref, in_sems, out_sems,
     perm, perm_t, uw, vw, field, adv1, adv2, edge1, edge2, xl, xr, ye, cl, cr,
-    gone, came, tv, flux_out, flux_in, sst_out, sst_in, back, home, mixed, spare,
+    gone, came, tv, flux_out, flux_in, sst_out, sst_in, back, mixed, spare,
     halo_send, halo_recv, tv_send, tv_recv, flux_send, flux_recv, sst_send, sst_recv,
     go_send, go_recv, back_send, back_recv,
     mid, mid2, plane, mid_send, mid_recv, stay_sem, home_send, home_recv, home_stay,
@@ -171,47 +182,19 @@
     for device in near:
         greet(device)
 
+    tall, wide = (CH, LANES), (1, LANES)
     for q in range(NQ):
-        wide = (CH, LANES)
         to = iota(wide, 1) + q * LANES
         perm[:, q * LANES:(q + 1) * LANES] = jnp.where(
-            iota(wide, 0) == lax.rem(to, HL) * NF + to // HL, F32(1), F32(0)
-        ).astype(BF16)
-        perm_t[:, q * LANES:(q + 1) * LANES] = jnp.where(
-            to == lax.rem(iota(wide, 0), HL) * NF + iota(wide, 0) // HL, F32(1), F32(0)
+            iota(tall, 0) == (to & (HL - 1)) * NF + (to >> 6), F32(1), F32(0)
         ).astype(BF16)
     for c in loads[:3]:
         c.wait()
-    hi, lo = split2(state_ref[...])
-    field[...] = dot(hi, perm[...]) + dot(lo, perm[...])
+    field[...] = dot_rows(state_ref[...], perm[...])
     for ref, wind in ((uw, u_ref), (vw, v_ref)):
         w = F32(0.1) * wind[...]
         ref[...] = jnp.concatenate([w, w], axis=1)
 
-    for c in loads[3:]:
-        c.wait()
-
-    square = (COLS, COLS)
-    hot_t = jnp.where(iota(square, 0) == order_ref[...], F32(1), F32(0))
-    hot = hot_t.T.astype(BF16)
-    hot_t = hot_t.astype(BF16)
-
-    mt = mixing_ref[...].T
-    lane = iota((HL, LANES), 1)
-    blocks = []
-    for li in range(2):
-        part = mt[li * HL:(li + 1) * HL]
-        turned = pltpu.roll(part, HL, axis=1)
-        zero = jnp.zeros_like(part)
-        blocks.append(jnp.concatenate([jnp.where(lane < HL, part, zero), jnp.where(lane < HL, turned, zero)], axis=1))
-        blocks.append(jnp.concatenate([jnp.where(lane < HL, zero, turned), jnp.where(lane < HL, zero, part)], axis=1))
-    pair_hi, pair_lo = split2(jnp.concatenate(blocks, axis=0))
-
-    sea = sea_ref[...].astype(F32)
-    weigh = jnp.zeros(square, F32)
-    for m in range(4):
-        weigh = weigh + jnp.where(iota(square, 0) == index_ref[m:m + 1, :], weight_ref[m:m + 1, :], F32(0))
-    calm = jnp.dot(omix_ref[...], temp_ref[...], precision=HIGH, preferred_element_type=F32)
 
     sends = []
 
@@ -250,6 +233,37 @@
     first = [exchange(0, part) for part in range(2)]
     for device in along_y:
         pl.semaphore_signal(plane, inc=1, device_id=device, device_id_type=MESH)
+    source = iota(tall, 0)
+    source = (source & (HL - 1)) * NF + (source >> 6)
+    for q in range(NQ):
+        perm_t[:, q * LANES:(q + 1) * LANES] = jnp.where(
+            source == iota(wide, 1) + q * LANES, F32(1), F32(0)
+        ).astype(BF16)
+    for c in loads[3:]:
+        c.wait()
+
+    square = (COLS, COLS)
+    hot_t = jnp.where(iota(square, 0) == order_ref[...], F32(1), F32(0))
+    hot = hot_t.T.astype(BF16)
+
+    mt = mixing_ref[...].T
+    lane = iota((HL, LANES), 1)
+    blocks = []
+    for li in range(2):
+        part = mt[li * HL:(li + 1) * HL]
+        turned = pltpu.roll(part, HL, axis=1)
+        zero = jnp.zeros_like(part)
+        blocks.append(jnp.concatenate([jnp.where(lane < HL, part, zero), jnp.where(lane < HL, turned, zero)], axis=1))
+        blocks.append(jnp.concatenate([jnp.where(lane < HL, zero, turned), jnp.where(lane < HL, zero, part)], axis=1))
+    pair_hi, pair_lo = split2(jnp.concatenate(blocks, axis=0))
+
+    sea = sea_ref[...].astype(F32)
+    weigh = jnp.zeros(square, F32)
+    for m in range(4):
+        weigh = weigh + jnp.where(iota(square, 0) == index_ref[m:m + 1, :], weight_ref[m:m + 1, :], F32(0))
+    calm = jnp.dot(omix_ref[...], temp_ref[...], precision=HIGH, preferred_element_type=F32)
+
+
     second = []
     for part in range(2):
         settle(0, part, first[part])
@@ -281,10 +295,9 @@
             sends.append(tv_copy)
         lanes = slice(part * CH // 2, (part + 1) * CH // 2)
         cut = pl.ds(part * CH // 2, CH // 2)
-        hi, lo = split2(field[:, lanes])
-        gone[:, lanes] = dot(hot, hi) + dot(hot, lo)
+        gone[:, lanes] = pick_rows(hot, field[:, lanes])
         for c in range(4):
-            turned = lax.rem(pair + c, 4)
+            turned = lax.rem(pair + PAIRS[c], 4)
             for d in range(3):
                 copy = remote(
                     gone.at[block(lax.rem(bx + d + 1, 4), turned), cut], mid.at[bx, rows_of(turned), cut],
@@ -308,22 +321,22 @@
                 copy.wait_recv()
 
         def send_columns(j, carry, c=c):
-            place, h = in_pair(c, j)
+            place, h = in_pair(PAIRS[c], j)
             remote(
                 both_x(mid, h, place), both_x(came, l, here), go_send, go_recv.at[c], (s, bx * 32 + place, h)
             ).start()
             return carry
 
-        lax.fori_loop(1 if c == 0 else 0, 16, send_columns, 0, unroll=True)
-        if c == 0:
-            pltpu.make_async_copy(both_x(mid, l, here), both_x(came, l, here), go_recv.at[0]).start()
+        lax.fori_loop(0 if PAIRS[c] else 1, 16, send_columns, 0, unroll=True)
+        if PAIRS[c] == 0:
+            pltpu.make_async_copy(both_x(mid, l, here), both_x(came, l, here), go_recv.at[c]).start()
             pltpu.make_async_copy(both_x(mid, l, here), spare.at[0], go_send).start()
 
     lane64 = iota((64, LANES), 1)
     for step in range(2):
         turns = []
         for c in (step * 2, step * 2 + 1):
-            turns.append(lax.rem(pair + 4 - c, 4))
+            turns.append(lax.rem(pair + 4 - PAIRS[c], 4))
             arrived = came.at[:, rows_of(turns[-1])]
             pltpu.make_async_copy(arrived, arrived, go_recv.at[c]).wait()
         loaded = [came[:, rows_of(t), :] for t in turns]
@@ -353,8 +366,7 @@
         condense = jnp.maximum(vapour - 0.5 * jnp.exp(0.3 * temper), 0.0)
         mixed[:, 0:LANES] = jnp.where(lane64 < HL, temper + 0.5 * condense, temper)
         mixed[:, LANES:2 * LANES] = jnp.where(lane64 < HL, vapour - condense, vapour)
-        hi, lo = split2(mixed[...])
-        ready = dot(hi, perm_t[...]) + dot(lo, perm_t[...])
+        ready = dot_rows(mixed[...], perm_t[...])
         for n, t in enumerate(turns):
             for h in range(2):
                 for x in range(2):
@@ -364,57 +376,36 @@
         for n, t in enumerate(turns):
             for x in range(2):
                 rate_ref[block(x, t), :] = rate[n * 16 + x * 8:n * 16 + x * 8 + 8]
-        for c in (step * 2, step * 2 + 1):
-
-            def send_rows(j, carry, c=c):
-                place, k = in_pair((4 - c) % 4, j)
+        for j in range(16):
+            for c in (step * 2, step * 2 + 1):
+                place, k = in_pair((4 - PAIRS[c]) % 4, j)
+                if j == 0 and PAIRS[c] == 0:
+                    pltpu.make_async_copy(both_x(back, l, here), both_x(mid2, l, here), back_recv.at[c]).start()
+                    pltpu.make_async_copy(both_x(back, l, here), spare.at[1], back_send).start()
+                    continue
                 remote(
                     both_x(back, k, place), both_x(mid2, l, here), back_send, back_recv.at[c], (s, bx * 32 + place, k)
                 ).start()
-                return carry
-
-            lax.fori_loop(1 if c == 0 else 0, 16, send_rows, 0, unroll=True)
-            if c == 0:
-                pltpu.make_async_copy(both_x(back, l, here), both_x(mid2, l, here), back_recv.at[0]).start()
-                pltpu.make_async_copy(both_x(back, l, here), spare.at[1], back_send).start()
-
-    tv_copy.wait_recv()
-    whole = jnp.concatenate([tv[0], tv[1]], axis=1)
-    both = dot3(whole, pair_hi, pair_lo)
-    level = lax.rem(lane128, HL)
-    total = jnp.zeros((COLS, LANES), F32)
-    for lo_ in range(2):
-        part = both[:, lo_ * LANES:(lo_ + 1) * LANES]
-        vapour = pltpu.roll(part, HL, axis=1)
-        condense = jnp.maximum(vapour - 0.5 * jnp.exp(0.3 * part), 0.0)
-        heat = part + 0.5 * condense
-        moist = vapour - condense
-        w = (1.0 + (level + lo_ * HL).astype(F32) / LEV) / math.sqrt(LEV)
-        total = total + jnp.where(lane128 < HL, w * (0.5 * heat + 0.5 * moist), 0.0)
-    flux = jnp.sum(total.T, axis=0, keepdims=True)
-    flux_out[...] = jnp.broadcast_to(flux, (8, LANES))
-    flux_copy = remote(flux_out, flux_in, flux_send, flux_recv, (1 - s, b, l))
-    flux_copy.start()
-    sends.append(flux_copy)
-
-    def pass_rows(c):
-        turned = lax.rem(pair + c, 4)
-        arrived = mid2.at[:, rows_of(turned)]
-        pltpu.make_async_copy(arrived, arrived, back_recv.at[c]).wait()
-        for d in range(3):
-            copy = remote(
-                mid2.at[lax.rem(bx + d + 1, 4), rows_of(turned)], home.at[block(bx, turned)],
-                home_send.at[c, d], home_recv.at[c, d], along_x[d],
-            )
-            copy.start()
-            last.append(copy)
-        copy = pltpu.make_async_copy(mid2.at[bx, rows_of(turned)], home.at[block(bx, turned)], home_stay.at[c])
-        copy.start()
-        stays.append(copy)
-
-    last, stays = [], []
-    pass_rows(0)
-    pass_rows(1)
+
+        if step == 0:
+            tv_copy.wait_recv()
+            whole = jnp.concatenate([tv[0], tv[1]], axis=1)
+            both = dot3(whole, pair_hi, pair_lo)
+            level = lax.rem(lane128, HL)
+            total = jnp.zeros((COLS, LANES), F32)
+            for lo_ in range(2):
+                part = both[:, lo_ * LANES:(lo_ + 1) * LANES]
+                vapour = pltpu.roll(part, HL, axis=1)
+                condense = jnp.maximum(vapour - 0.5 * jnp.exp(0.3 * part), 0.0)
+                heat = part + 0.5 * condense
+                moist = vapour - condense
+                w = (1.0 + (level + lo_ * HL).astype(F32) / LEV) / math.sqrt(LEV)
+                total = total + jnp.where(lane128 < HL, w * (0.5 * heat + 0.5 * moist), 0.0)
+            flux = jnp.sum(total.T, axis=0, keepdims=True)
+            flux_out[...] = jnp.broadcast_to(flux, (8, LANES))
+            flux_copy = remote(flux_out, flux_in, flux_send, flux_recv, (1 - s, b, l))
+            flux_copy.start()
+            sends.append(flux_copy)
 
     flux_copy.wait_recv()
     forcing = jnp.dot(flux_in[...], weigh, precision=HIGH, preferred_element_type=F32)
@@ -431,8 +422,6 @@
     for c in sst_copies:
         c.start()
 
-    pass_rows(2)
-    pass_rows(3)
     for h in range(2):
         rows_ref[:, h * CH:(h + 1) * CH] = back[h * 2:h * 2 + 2].reshape(64, CH)
 
@@ -442,6 +431,26 @@
         return c
 
     stores = [store(0, rate_ref, rate_hbm), store(1, rows_ref, rows_hbm), store(2, curves_ref, curves_hbm)]
+
+
+    def pass_rows(c):
+        turned = lax.rem(pair + PAIRS[c], 4)
+        arrived = mid2.at[:, rows_of(turned)]
+        pltpu.make_async_copy(arrived, arrived, back_recv.at[c]).wait()
+        for d in range(3):
+            copy = remote(
+                mid2.at[lax.rem(bx + d + 1, 4), rows_of(turned)], home.at[block(bx, turned)],
+                home_send.at[c, d], home_recv.at[c, d], along_x[d],
+            )
+            copy.start()
+            last.append(copy)
+        copy = pltpu.make_async_copy(mid2.at[bx, rows_of(turned)], home.at[block(bx, turned)], home_stay.at[c])
+        copy.start()
+        stays.append(copy)
+
+    last, stays = [], []
+    for c in range(4):
+        pass_rows(c)
 
     for k in range(2):
         remote(sst_out, sst_in.at[k], sst_send.at[k], sst_recv.at[k], (1 - s, b, k)).wait_recv()
@@ -451,18 +460,13 @@
     pick = jnp.where(lax.rem(iota((COLS, NY), 0), NY) == iota((COLS, NY), 1), F32(1), F32(0))
     sst_ref[...] = jnp.dot(surface, pick, precision=HIGH, preferred_element_type=F32)
 
-    stores.append(store(4, sst_ref, sst_hbm))
+    stores.append(store(3, sst_ref, sst_hbm))
 
     for c in stays:
         c.wait()
     for c in last:
         c.wait_recv()
     sends += last
-    hi, lo = split2(home[...])
-    adv_ref[...] = dot(hot_t, hi) + dot(hot_t, lo)
-
-    stores.append(store(3, adv_ref, adv_hbm))
-
     pltpu.make_async_copy(mid, came, go_send).wait()
     pltpu.make_async_copy(back, mid2, back_send).wait()
     for c in sends:
@@ -474,14 +478,21 @@
 
 
 def hand_over(*refs):
-    src, dst, held, sems = refs[:5], refs[5:10], refs[10:15], refs[15]
+    order_hbm, src, dst, order_ref, held, out_ref, sems = refs[0], refs[1:6], refs[6:11], refs[11], refs[12:17], refs[17], refs[18]
     loads = [pltpu.make_async_copy(src[i], held[i], sems.at[0, i]) for i in range(5)]
-    stores = [pltpu.make_async_copy(held[i], dst[i], sems.at[1, i]) for i in range(5)]
+    order = pltpu.make_async_copy(order_hbm, order_ref, sems.at[0, 5])
+    stores = [pltpu.make_async_copy(held[i] if i else out_ref, dst[i], sems.at[1, i]) for i in range(5)]
+    order.start()
     for c in loads:
         c.start()
-    for a, b in zip(loads, stores):
-        a.wait()
-        b.start()
+    order.wait()
+    hot_t = jnp.where(iota((COLS, COLS), 0) == order_ref[...], F32(1), F32(0)).astype(BF16)
+    loads[0].wait()
+    out_ref[...] = pick_rows(hot_t, held[0][...])
+    for i in range(5):
+        if i:
+            loads[i].wait()
+        stores[i].start()
     for c in stores:
         c.wait()
 
@@ -505,7 +516,7 @@
         pltpu.VMEM((2, COLS, LANES), F32),
         pltpu.VMEM((8, LANES), F32), pltpu.VMEM((8, LANES), F32),
         pltpu.VMEM((8, LANES), F32), pltpu.VMEM((2, 8, LANES), F32),
-        split, big, pltpu.VMEM((64, CH), F32),
+        split, pltpu.VMEM((64, CH), F32),
         pltpu.VMEM((2, 2, 1, CH), F32),
         dma((2, 2, 5)), dma((2, 2, 5)), dma, dma, dma, dma, dma((2,)), dma((2,)),
         dma, dma((4,)), dma, dma((4,)),
@@ -531,13 +542,13 @@
         ocean_temp,
         ocean_mixing,
     )
-    held = [pltpu.VMEM(a.shape, a.dtype) for a in (*ins, *out_shape)]
+    held = [pltpu.VMEM(a.shape, a.dtype) for a in (*ins, *out_shape[1:])]
     outs = pl.pallas_call(
         window_kernel,
         out_shape=out_shape,
         in_specs=[hbm] * 10,
         out_specs=[hbm] * 5,
-        scratch_shapes=[*held, dma((10,)), dma((5,)), *scratch],
+        scratch_shapes=[*held, dma((10,)), dma((4,)), *scratch],
         compiler_params=pltpu.CompilerParams(
             collective_id=0, has_side_effects=True, vmem_limit_bytes=56 * 2**20
         ),
@@ -546,12 +557,14 @@
     outs = pl.pallas_call(
         hand_over,
         out_shape=out_shape,
-        in_specs=[hbm] * 5,
+        in_specs=[hbm] * 6,
         out_specs=[hbm] * 5,
-        scratch_shapes=[*(pltpu.VMEM(a.shape, a.dtype) for a in out_shape), dma((2, 5))],
+        scratch_shapes=[
+            pltpu.VMEM((1, COLS), jnp.int32), *(pltpu.VMEM(a.shape, a.dtype) for a in out_shape), big, dma((2, 6))
+        ],
         compiler_params=pltpu.CompilerParams(vmem_limit_bytes=56 * 2**20),
         name="outputs",
-    )(*outs)
+    )(ins[4], *outs)
     return (outs[0].reshape(state.shape), *outs[1:])
 
 

time: 63.4 us -> 60.9 us (0.961)
  Pallas kernels: 62.6 us -> 60.1 us
    pallas_call x1, Pallas kernels: 60.6 us -> 57.8 us  [on_device(): pl.pallas_call(window_kernel, out_shape=out_shape, in_specs=[hbm] * 10, o...]
where the time goes in v4:
time: 60.9 us; the launch traced here: 60.7 us
  Pallas kernels  60.1 us (99%)
  between operations  0.64 us (1%)
    pallas_call x1, Pallas kernels, on_device(): pl.pallas_call(window_kernel, out_shape=out_shape, in_specs=[hbm] * 10, o...  57.8 us
    pallas_call x1, Pallas kernels, on_device(): pl.pallas_call(hand_over, out_shape=out_shape, in_specs=[hbm] * 6, out_sp...  2.23 us

profile of v4, /device:TPU:1, one launch (start us, length us, event | category | flops | bytes accessed | tf_op | source)
XLA Modules:
  0.0 60.7 jit_solution(15288677939004679264)
XLA Ops:
  0.6 57.8 %window.1 = (f32[128,768]{1,0:T(8,128)}, f32[64,128]{1,0:T(8,128)}, f32[64,1536]{1,0:T(8,128)}, f32[80,128]{1,0:T(8,128)}, f32[8,16]{1,0:T(8,128)}) custom-call(f32[128,768]{1,0:T(8,128)} %bitcast.8, f32[128,64]{1,0:T(8,128)} %bitcast.9, f32[128,64]{1,0:T(8,128)} %bitcast.10, f32[128,128]{1,0:T(8,128)} %mixing_hbm.1, s32[1,128]{1,0:T(1,128)} %bitcast.13, ...), custom_call_target="tpu_custom_call" | custom-call | tf_op jit(solution)/shard_map/window/pallas_call | solution.py:546
  58.5 2.2 %outputs.1 = (f32[128,768]{1,0:T(8,128)}, f32[64,128]{1,0:T(8,128)}, f32[64,1536]{1,0:T(8,128)}, f32[80,128]{1,0:T(8,128)}, f32[8,16]{1,0:T(8,128)}) custom-call(s32[1,128]{1,0:T(1,128)} %bitcast.14, f32[128,768]{1,0:T(8,128)} %get-tuple-element.15.refs_1_, f32[64,128]{1,0:T(8,128)} %get-tuple-element.16.refs_2_, f32[64,1536]{1,0:T(8,128)} %get-tuple-element.17.refs_3_, ...), custom_call_target="tpu_custom_call" | custom-call | tf_op jit(solution)/shard_map/outputs/pallas_call | solution.py:557

commit v5 on v4

--- a/solution.py
+++ b/solution.py
@@ -163,7 +163,7 @@
             (index_hbm, index_ref), (weight_hbm, weight_ref), (sea_hbm, sea_ref), (temp_hbm, temp_ref), (omix_hbm, omix_ref),
         ))
     ]
-    for c in loads:
+    for c in loads[:3]:
         c.start()
 
     barrier = pltpu.get_barrier_semaphore()
@@ -181,6 +181,9 @@
     near += along_x + along_z + along_y
     for device in near:
         greet(device)
+
+    for c in loads[3:]:
+        c.start()
 
     tall, wide = (CH, LANES), (1, LANES)
     for q in range(NQ):
@@ -280,8 +283,8 @@
         return pl.ds(pl.multiple_of(x * 32 + turned * 8, 8), 8)
 
     def in_pair(c, j):
-        y = lax.rem(pair + c, 4) * 2 + lax.rem(by + j // 8, 2)
-        return y * 4 + lax.rem(bz + j // 2, 4), lax.rem(l + j, 2)
+        y = lax.rem(pair + c, 4) * 2 + lax.rem(by + j, 2)
+        return y * 4 + lax.rem(bz + j // 4, 4), lax.rem(l + j // 2, 2)
 
     across = []
     for part in range(2):
@@ -331,6 +334,25 @@
         if PAIRS[c] == 0:
             pltpu.make_async_copy(both_x(mid, l, here), both_x(came, l, here), go_recv.at[c]).start()
             pltpu.make_async_copy(both_x(mid, l, here), spare.at[0], go_send).start()
+
+    tv_copy.wait_recv()
+    whole = jnp.concatenate([tv[0], tv[1]], axis=1)
+    both = dot3(whole, pair_hi, pair_lo)
+    level = lax.rem(lane128, HL)
+    total = jnp.zeros((COLS, LANES), F32)
+    for lo_ in range(2):
+        part = both[:, lo_ * LANES:(lo_ + 1) * LANES]
+        vapour = pltpu.roll(part, HL, axis=1)
+        condense = jnp.maximum(vapour - 0.5 * jnp.exp(0.3 * part), 0.0)
+        heat = part + 0.5 * condense
+        moist = vapour - condense
+        w = (1.0 + (level + lo_ * HL).astype(F32) / LEV) / math.sqrt(LEV)
+        total = total + jnp.where(lane128 < HL, w * (0.5 * heat + 0.5 * moist), 0.0)
+    flux = jnp.sum(total.T, axis=0, keepdims=True)
+    flux_out[...] = jnp.broadcast_to(flux, (8, LANES))
+    flux_copy = remote(flux_out, flux_in, flux_send, flux_recv, (1 - s, b, l))
+    flux_copy.start()
+    sends.append(flux_copy)
 
     lane64 = iota((64, LANES), 1)
     for step in range(2):
@@ -386,26 +408,6 @@
                 remote(
                     both_x(back, k, place), both_x(mid2, l, here), back_send, back_recv.at[c], (s, bx * 32 + place, k)
                 ).start()
-
-        if step == 0:
-            tv_copy.wait_recv()
-            whole = jnp.concatenate([tv[0], tv[1]], axis=1)
-            both = dot3(whole, pair_hi, pair_lo)
-            level = lax.rem(lane128, HL)
-            total = jnp.zeros((COLS, LANES), F32)
-            for lo_ in range(2):
-                part = both[:, lo_ * LANES:(lo_ + 1) * LANES]
-                vapour = pltpu.roll(part, HL, axis=1)
-                condense = jnp.maximum(vapour - 0.5 * jnp.exp(0.3 * part), 0.0)
-                heat = part + 0.5 * condense
-                moist = vapour - condense
-                w = (1.0 + (level + lo_ * HL).astype(F32) / LEV) / math.sqrt(LEV)
-                total = total + jnp.where(lane128 < HL, w * (0.5 * heat + 0.5 * moist), 0.0)
-            flux = jnp.sum(total.T, axis=0, keepdims=True)
-            flux_out[...] = jnp.broadcast_to(flux, (8, LANES))
-            flux_copy = remote(flux_out, flux_in, flux_send, flux_recv, (1 - s, b, l))
-            flux_copy.start()
-            sends.append(flux_copy)
 
     flux_copy.wait_recv()
     forcing = jnp.dot(flux_in[...], weigh, precision=HIGH, preferred_element_type=F32)

time: 60.9 us -> 59.8 us (0.982)
  Pallas kernels: 60.1 us -> 58.8 us
    pallas_call x1, Pallas kernels: 57.8 us -> 56.6 us  [on_device(): pl.pallas_call(window_kernel, out_shape=out_shape, in_specs=[hbm] * 10, o...]
where the time goes in v5:
time: 59.8 us; the launch traced here: 59.4 us
  Pallas kernels  58.8 us (98%)
  between operations  0.64 us (1%)
    pallas_call x1, Pallas kernels, on_device(): pl.pallas_call(window_kernel, out_shape=out_shape, in_specs=[hbm] * 10, o...  56.6 us
    pallas_call x1, Pallas kernels, on_device(): pl.pallas_call(hand_over, out_shape=out_shape, in_specs=[hbm] * 6, out_sp...  2.23 us

profile of v5, /device:TPU:1, one launch (start us, length us, event | category | flops | bytes accessed | tf_op | source)
XLA Modules:
  0.0 59.4 jit_solution(18040648529487376865)
XLA Ops:
  0.6 56.6 %window.1 = (f32[128,768]{1,0:T(8,128)}, f32[64,128]{1,0:T(8,128)}, f32[64,1536]{1,0:T(8,128)}, f32[80,128]{1,0:T(8,128)}, f32[8,16]{1,0:T(8,128)}) custom-call(f32[128,768]{1,0:T(8,128)} %bitcast.8, f32[128,64]{1,0:T(8,128)} %bitcast.9, f32[128,64]{1,0:T(8,128)} %bitcast.10, f32[128,128]{1,0:T(8,128)} %mixing_hbm.1, s32[1,128]{1,0:T(1,128)} %bitcast.13, ...), custom_call_target="tpu_custom_call" | custom-call | tf_op jit(solution)/shard_map/window/pallas_call | solution.py:548
  57.2 2.2 %outputs.1 = (f32[128,768]{1,0:T(8,128)}, f32[64,128]{1,0:T(8,128)}, f32[64,1536]{1,0:T(8,128)}, f32[80,128]{1,0:T(8,128)}, f32[8,16]{1,0:T(8,128)}) custom-call(s32[1,128]{1,0:T(1,128)} %bitcast.14, f32[128,768]{1,0:T(8,128)} %get-tuple-element.15.refs_1_, f32[64,128]{1,0:T(8,128)} %get-tuple-element.16.refs_2_, f32[64,1536]{1,0:T(8,128)} %get-tuple-element.17.refs_3_, ...), custom_call_target="tpu_custom_call" | custom-call | tf_op jit(solution)/shard_map/outputs/pallas_call | solution.py:559

commit v6 on v5

--- a/solution.py
+++ b/solution.py
@@ -481,21 +481,26 @@
 
 def hand_over(*refs):
     order_hbm, src, dst, order_ref, held, out_ref, sems = refs[0], refs[1:6], refs[6:11], refs[11], refs[12:17], refs[17], refs[18]
-    loads = [pltpu.make_async_copy(src[i], held[i], sems.at[0, i]) for i in range(5)]
-    order = pltpu.make_async_copy(order_hbm, order_ref, sems.at[0, 5])
-    stores = [pltpu.make_async_copy(held[i] if i else out_ref, dst[i], sems.at[1, i]) for i in range(5)]
+    cuts = [pl.ds(i * CH // 3, CH // 3) for i in range(3)]
+    order = pltpu.make_async_copy(order_hbm, order_ref, sems.at[0, 0])
+    loads = [pltpu.make_async_copy(src[0].at[:, cut], held[0].at[:, cut], sems.at[0, 5 + i]) for i, cut in enumerate(cuts)]
+    stores = [pltpu.make_async_copy(out_ref.at[:, cut], dst[0].at[:, cut], sems.at[1, 5 + i]) for i, cut in enumerate(cuts)]
+    others = [pltpu.make_async_copy(src[i], held[i], sems.at[0, i]) for i in range(1, 5)]
+    results = [pltpu.make_async_copy(held[i], dst[i], sems.at[1, i]) for i in range(1, 5)]
     order.start()
-    for c in loads:
+    for c in loads + others:
         c.start()
     order.wait()
     hot_t = jnp.where(iota((COLS, COLS), 0) == order_ref[...], F32(1), F32(0)).astype(BF16)
-    loads[0].wait()
-    out_ref[...] = pick_rows(hot_t, held[0][...])
-    for i in range(5):
-        if i:
-            loads[i].wait()
+    for i in range(3):
+        loads[i].wait()
+        lanes = slice(i * CH // 3, (i + 1) * CH // 3)
+        out_ref[:, lanes] = pick_rows(hot_t, held[0][:, lanes])
         stores[i].start()
-    for c in stores:
+    for a, b in zip(others, results):
+        a.wait()
+        b.start()
+    for c in stores + results:
         c.wait()
 
 
@@ -562,7 +567,7 @@
         in_specs=[hbm] * 6,
         out_specs=[hbm] * 5,
         scratch_shapes=[
-            pltpu.VMEM((1, COLS), jnp.int32), *(pltpu.VMEM(a.shape, a.dtype) for a in out_shape), big, dma((2, 6))
+            pltpu.VMEM((1, COLS), jnp.int32), *(pltpu.VMEM(a.shape, a.dtype) for a in out_shape), big, dma((2, 8))
         ],
         compiler_params=pltpu.CompilerParams(vmem_limit_bytes=56 * 2**20),
         name="outputs",

time: 59.8 us -> 60 us (level)
  no operation moved by 1% of the time
where the time goes in v6:
time: 60 us; the launch traced here: 59.6 us
  Pallas kernels  59 us (98%)
  between operations  0.64 us (1%)
    pallas_call x1, Pallas kernels, on_device(): pl.pallas_call(window_kernel, out_shape=out_shape, in_specs=[hbm] * 10, o...  56.6 us
    pallas_call x1, Pallas kernels, on_device(): pl.pallas_call(hand_over, out_shape=out_shape, in_specs=[hbm] * 6, out_sp...  2.4 us

profile of v6, /device:TPU:1, one launch (start us, length us, event | category | flops | bytes accessed | tf_op | source)
XLA Modules:
  0.0 59.6 jit_solution(4916957517957843675)
XLA Ops:
  0.6 56.6 %window.1 = (f32[128,768]{1,0:T(8,128)}, f32[64,128]{1,0:T(8,128)}, f32[64,1536]{1,0:T(8,128)}, f32[80,128]{1,0:T(8,128)}, f32[8,16]{1,0:T(8,128)}) custom-call(f32[128,768]{1,0:T(8,128)} %bitcast.8, f32[128,64]{1,0:T(8,128)} %bitcast.9, f32[128,64]{1,0:T(8,128)} %bitcast.10, f32[128,128]{1,0:T(8,128)} %mixing_hbm.1, s32[1,128]{1,0:T(1,128)} %bitcast.13, ...), custom_call_target="tpu_custom_call" | custom-call | tf_op jit(solution)/shard_map/window/pallas_call | solution.py:553
  57.2 2.4 %outputs.1 = (f32[128,768]{1,0:T(8,128)}, f32[64,128]{1,0:T(8,128)}, f32[64,1536]{1,0:T(8,128)}, f32[80,128]{1,0:T(8,128)}, f32[8,16]{1,0:T(8,128)}) custom-call(s32[1,128]{1,0:T(1,128)} %bitcast.14, f32[128,768]{1,0:T(8,128)} %get-tuple-element.15.refs_1_, f32[64,128]{1,0:T(8,128)} %get-tuple-element.16.refs_2_, f32[64,1536]{1,0:T(8,128)} %get-tuple-element.17.refs_3_, ...), custom_call_target="tpu_custom_call" | custom-call | tf_op jit(solution)/shard_map/outputs/pallas_call | solution.py:564
